TPU v7x, 128 devices: a whole 4x4x4 slice. The times are simulated.
128 devices in a mesh: chan: 32 (over z, y, x_hi), tm: 4 (over x_lo, core).
Axes of the slice: x: 4 (x_hi: 2, x_lo: 2; x = x_hi * 2 + x_lo), y: 4, z: 4, core: 2. Of those that a mesh axis runs over, the one named last changes fastest.
Arguments:
- visibilities: bfloat16 [64, 16, 2, 512, 512], P('chan', 'tm'), may hold values from -640 to 640, as said below
- model: bfloat16 [64, 16, 2, 512, 512], P('chan', 'tm'), may hold values from -32 to 32, as said below
- beam_left: bfloat16 [8, 256, 128], replicated, may hold values from -0.5 to 0.5
- beam_right: bfloat16 [8, 256, 128], replicated, may hold values from -0.01171875 to 0.01171875
- weight_index: int32 [64, 16], P('chan'), may hold values from 0 to 7
- target_bank: int32 [64, 16, 16], P('chan', 'tm'), may hold values from 0 to 7
- widths: int32 [64], P('chan'), may hold values from 0 to 2, as said below
Outputs:
- covariance: float32 [4096, 256], P('chan')
Inputs may be any that keep to these rules, and one draw needn't show every extreme that they name: `visibilities`: real part at index 0 and imaginary part at index 1; each matrix is Hermitian in its last two dimensions. `model`: real part at index 0 and imaginary part at index 1; each matrix is Hermitian in its last two dimensions. `widths`: some channel has width 2.
All inputs are finite; a program needn't handle non-finite values.
Results may differ from a plain program's by a relative error of at most 0.0041.
Values sent between devices are 32-bit elements; how exact they have to be, the bound alone decides.
A program may use at most 256 MiB of HBM per device.

v0:
```python
import jax
import jax.numpy as jnp
from jax import lax
from jax.sharding import PartitionSpec as P

N = 512
BLK = 128
BEAMS = 256
BANKS = 8
ITERS = 6
HW = 2


epsilon = 1e-06


def extended_2(cells, sides, width):
    for axis, dim in sides:
        count = lax.axis_size(axis)
        ends = count - 1
        head = lax.slice_in_dim(cells, 0, width, axis=dim)
        tail = lax.slice_in_dim(cells, cells.shape[dim] - width, cells.shape[dim], axis=dim)
        cells = jnp.concatenate(
            [
                lax.ppermute(tail, axis, [(i, (i + 1) % count) for i in range(ends)]),
                cells,
                lax.ppermute(head, axis, [((i + 1) % count, i) for i in range(ends)]),
            ],
            axis=dim,
        )
    return cells


def contract_rows(vectors, matrix):
    return jnp.einsum("...kq,...qp->...kp", vectors, matrix, precision=lax.Precision.HIGHEST)


def stefcal(visibilities, model):
    vis_re = visibilities[..., 0, :, :].astype(jnp.float32)
    vis_im = visibilities[..., 1, :, :].astype(jnp.float32)
    mod_re = model[..., 0, :, :].astype(jnp.float32)
    mod_im = model[..., 1, :, :].astype(jnp.float32)
    cross_re = mod_re * vis_re + mod_im * vis_im
    cross_im = mod_im * vis_re - mod_re * vis_im
    power = mod_re * mod_re + mod_im * mod_im
    gain_re = jnp.ones(vis_re.shape[:-1], jnp.float32)
    gain_im = jnp.zeros(vis_re.shape[:-1], jnp.float32)
    for sweep_index in range(ITERS):
        paired = jnp.stack([gain_re, gain_im], axis=-2)
        with_real = contract_rows(paired, cross_re)
        with_imag = contract_rows(paired, cross_im)
        magnitude = (gain_re * gain_re + gain_im * gain_im)[..., None, :]
        denominator = contract_rows(magnitude, power)[..., 0, :] + epsilon
        num_re = with_real[..., 0, :] - with_imag[..., 1, :]
        num_im = with_imag[..., 0, :] + with_real[..., 1, :]
        new_re = num_re / denominator
        new_im = num_im / denominator
        if sweep_index % 2 == 1:
            gain_re = 0.5 * (new_re + gain_re)
            gain_im = 0.5 * (new_im + gain_im)
        else:
            gain_re = new_re
            gain_im = new_im
    return (gain_re, gain_im)


def align_phase(gain_re, gain_im):
    first_re = gain_re[..., :1]
    first_im = gain_im[..., :1]
    divisor = jnp.maximum(jnp.sqrt(first_re * first_re + first_im * first_im), 1.0)
    unit_re = first_re / divisor
    unit_im = -first_im / divisor
    return (gain_re * unit_re - gain_im * unit_im, gain_re * unit_im + gain_im * unit_re)


def calibrate(smooth_re, smooth_im, visibilities):
    vis_re = visibilities[..., 0, :, :].astype(jnp.float32)
    vis_im = visibilities[..., 1, :, :].astype(jnp.float32)
    denominator = jnp.maximum(smooth_re * smooth_re + smooth_im * smooth_im, 1.0)
    inv_re = smooth_re / denominator
    inv_im = -smooth_im / denominator
    row_re = inv_re[..., :, None]
    row_im = inv_im[..., :, None]
    col_re = inv_re[..., None, :]
    col_im = inv_im[..., None, :]
    left_re = row_re * vis_re - row_im * vis_im
    left_im = row_re * vis_im + row_im * vis_re
    out_re = left_re * col_re + left_im * col_im
    out_im = left_im * col_re - left_re * col_im
    return jnp.stack([out_re, out_im], axis=-3).astype(jnp.bfloat16)


def local(visibilities, model, beam_left, beam_right, weight_index, target_bank, widths):
    local_channels = visibilities.shape[0]
    local_intervals = visibilities.shape[1]
    group_count = N // BLK
    gain_re, gain_im = stefcal(visibilities, model)
    ref_re, ref_im = align_phase(gain_re, gain_im)
    stacked = jnp.stack([ref_re, ref_im], axis=2)
    extended = extended_2(stacked, (("tm", 1),), HW)
    interval = lax.axis_index("tm") * local_intervals + jnp.arange(local_intervals, dtype=jnp.int32)
    all_intervals = lax.axis_size("tm") * local_intervals
    summed = jnp.zeros_like(stacked)
    counts = jnp.zeros((local_channels, local_intervals), jnp.float32)
    for offset in range(-HW, HW + 1):
        inside = (
            (abs(offset) <= widths[:, None])
            & (interval[None, :] + offset >= 0)
            & (interval[None, :] + offset < all_intervals)
        ).astype(jnp.float32)
        summed = (
            summed
            + inside[:, :, None, None] * extended[:, HW + offset : HW + offset + local_intervals]
        )
        counts = counts + inside
    smooth = summed / counts[:, :, None, None]
    calibrated = calibrate(smooth[:, :, 0], smooth[:, :, 1], visibilities)
    pieces = calibrated.reshape(
        (local_channels, local_intervals, 2, group_count, BLK, group_count, BLK)
    )
    left_groups = beam_left[weight_index].reshape(
        (local_channels, group_count, group_count, BEAMS, BLK)
    )
    right_groups = beam_right[weight_index].reshape(
        (local_channels, group_count, group_count, BEAMS, BLK)
    )
    bank_hits = (target_bank[..., None] == jnp.arange(BANKS, dtype=jnp.int32)).astype(jnp.float32)
    bank_hits = bank_hits.reshape(
        (local_channels, local_intervals, group_count, group_count, BANKS)
    )

    def per_channel(accumulated, channel_data):
        piece_one, left_one, right_one, hits_one = channel_data
        formed = jnp.einsum(
            "ijux,tsixjy->tijsuy", left_one, piece_one, preferred_element_type=jnp.float32
        ).astype(jnp.bfloat16)
        contrib = jnp.einsum(
            "tijsuy,ijvy->tijsuv", formed, right_one, preferred_element_type=jnp.float32
        )
        accumulated = accumulated + jnp.einsum(
            "tijk,tijsuv->ksuv", hits_one, contrib, precision=lax.Precision.HIGHEST
        )
        return (accumulated, None)

    start_banks = jnp.zeros((BANKS, 2, BEAMS, BEAMS), jnp.float32)
    bank_terms, unused = lax.scan(
        per_channel, start_banks, (pieces, left_groups, right_groups, bank_hits)
    )
    bank_terms = bank_terms.reshape((BANKS * 2 * BEAMS, BEAMS))
    shares = lax.psum_scatter(bank_terms, "chan", scatter_dimension=0, tiled=True)
    result = lax.psum(shares, "tm")
    return result


def solution(mesh):
    return jax.shard_map(
        local,
        mesh=mesh,
        in_specs=(
            P("chan", "tm", None, None, None),
            P("chan", "tm", None, None, None),
            P(),
            P(),
            P("chan", None),
            P("chan", "tm", None),
            P("chan"),
        ),
        out_specs=P("chan", None),
        check_vma=False,
    )
```

profile of v0, /device:TPU:1, one launch (start us, length us, event | category | flops | bytes accessed | tf_op | source)
XLA Modules:
  0.0 616.5 jit_solution(4730646619423321307)
XLA Ops:
  6.5 7.7 %fusion.81 = f32[2,4,1,512]{3,2,1,0:T(1,128)S(1)} fusion(bf16[2,4,2,512,512]{4,3,2,1,0:T(8,128)(2,1)} %param.10), kind=kOutput, calls=%fused_computation.151 | convolution fusion | flops 35651584 | bytes 8404992 | tf_op jit(solution)/shard_map/...kq,...qp->...kp/dot_general | solution.py:35
  14.2 7.6 %fusion.20 = (f32[2,4,512,512]{3,2,1,0:T(8,128)S(1)}, f32[2,4,512,512]{3,2,1,0:T(8,128)S(1)}) fusion(bf16[2,4,2,512,512]{4,3,2,1,0:T(8,128)(2,1)} %param.10, bf16[2,4,2,512,512]{4,3,2,1,0:T(8,128)(2,1)} %param.9), kind=kLoop, calls=%fused_computation.30 | loop fusion | flops 20971520 | bytes 33554432 | tf_op jit(solution)/shard_map/add | solution.py:43
  52.4 5.3 fusion.75
  66.1 5.7 fusion.73
  80.0 6.2 fusion.71
  94.5 5.3 fusion.69
  110.4 9.3 %add_convert_fusion = (bf16[2,4,1,512,512]{4,3,2,1,0:T(8,128)(2,1)}, bf16[2,4,1,512,512]{4,3,2,1,0:T(8,128)(2,1)}) fusion(f32[2,4,512]{2,1,0:T(4,128)S(1)} %get-tuple-element.110, f32[2,4,512]{2,1,0:T(4,128)S(1)} %get-tuple-element.109, f32[2,4,512]{2,1,0:T(4,128)S(1)} %get-tuple-element.108, f32[2,4,512]{2,1,0:T(4,128)S(1)} %get-tuple-element.107, ...), kind=kLoop, calls=%fused_computation.37 | loop fusion | flops 33554432 | bytes 16842752 | tf_op jit(solution)/shard_map/convert.3
  119.7 6.9 %stack.45 = bf16[2,4,1,4,128,4,128]{6,5,4,3,1,0,2:T(4,128)(2,1)} reshape(bf16[2,4,1,512,512]{4,3,2,1,0:T(8,128)(2,1)} %get-tuple-element.105) | data formatting | bytes 8388608 | tf_op jit(solution)/shard_map/stack | solution.py:90
  126.6 6.9 %stack.46 = bf16[2,4,1,4,128,4,128]{6,5,4,3,1,0,2:T(4,128)(2,1)} reshape(bf16[2,4,1,512,512]{4,3,2,1,0:T(8,128)(2,1)} %get-tuple-element.106) | data formatting | bytes 8388608 | tf_op jit(solution)/shard_map/stack | solution.py:90
  133.5 8.7 %pad_maximum_fusion = bf16[2,4,2,4,128,4,128]{6,5,4,3,1,0,2:T(4,128)(2,1)} fusion(bf16[2,4,1,4,128,4,128]{6,5,4,3,1,0,2:T(4,128)(2,1)} %stack.46, bf16[2,4,1,4,128,4,128]{6,5,4,3,1,0,2:T(4,128)(2,1)} %stack.45), kind=kLoop, calls=%fused_computation.35 | loop fusion | flops 4194304 | bytes 16777216 | tf_op jit(solution)/shard_map/stack | solution.py:90
  142.2 226.3 %while.11 = (s32[]{:T(128)}, f32[8,2,256,256]{3,0,2,1:T(8,128)}, f32[2,4,4,4,8]{4,1,3,2,0:T(4,128)S(1)}, bf16[2,4,4,256,128]{4,3,2,1,0:T(8,128)(2,1)S(1)}, bf16[...) while((s32[]{:T(128)}, f32[8,2,256,256]{3,0,2,1:T(8,128)}, ...), condition=%wide.region_1.2_spmd.clone, body=%wide.region_0.1_spmd.clone.sunk | while | flops 4032823296 | bytes 165708912 | solution.py:146
  142.4 6.7 %constant_dynamic-slice_fusion.2 = bf16[1,4,2,4,128,4,128]{6,5,4,3,1,0,2:T(4,128)(2,1)} fusion(bf16[2,4,2,4,128,4,128]{6,5,4,3,1,0,2:T(4,128)(2,1)} %get-tuple-element.215, s32[]{:T(128)} %get-tuple-element.203), kind=kLoop, calls=%fused_computation.15.clone.1 | loop fusion | bytes 8388612 | tf_op jit(solution)/shard_map/while/body/jit(dynamic_index_in_dim)/dynamic_slice | solution.py:146
  149.1 7.5 %copy.392 = bf16[1,4,2,4,128,4,128]{4,6,2,1,5,3,0:T(8,128)(2,1)} copy(bf16[1,4,2,4,128,4,128]{6,5,4,3,1,0,2:T(4,128)(2,1)} %constant_dynamic-slice_fusion.2) | data formatting | bytes 8388608 | tf_op jit(solution)/shard_map/while/body/jit(dynamic_index_in_dim)/dynamic_slice | solution.py:146
  156.6 15.9 %convolution_bitcast_fusion.2 = f32[4,4,4,2,256,256]{4,5,3,0,2,1:T(8,128)} fusion(bf16[1,4,2,4,128,4,128]{4,6,2,1,5,3,0:T(8,128)(2,1)} %copy.392, bf16[2,4,4,256,128]{4,3,2,1,0:T(8,128)(2,1)} %get-tuple-element.216, s32[]{:T(128)} %get-tuple-element.203, bf16[2,4,4,256,128]{4,3,2,1,0:T(8,128)(2,1)S(1)} %get-tuple-element.214), kind=kOutput, calls=%fused_computation.2.clone.1 | convolution fusion | flops 3225419776 | bytes 39846912 | tf_op jit(solution)/shard_map/while/body/eval_jaxpr/tijsuy,ijvy->tijsuv/dot_general | solution.py:137
  172.5 39.9 %copy.393 = f32[4,4,4,2,256,256]{5,0,2,1,4,3:T(4,128)} copy(f32[4,4,4,2,256,256]{4,5,3,0,2,1:T(8,128)} %convolution_bitcast_fusion.2) | data formatting | bytes 67108864 | tf_op jit(solution)/shard_map/while/body/eval_jaxpr/tijsuy,ijvy->tijsuv/transpose | solution.py:137
  212.4 42.9 %bitcast_add_fusion.10 = f32[8,2,256,256]{3,0,2,1:T(8,128)} fusion(f32[8,2,256,256]{3,0,2,1:T(8,128)} %get-tuple-element.204, f32[4,4,4,2,256,256]{5,0,2,1,4,3:T(4,128)} %copy.393, pred[]{:T(512)S(6)} %compare.3, f32[2,4,4,4,8]{4,1,3,2,0:T(4,128)S(1)} %get-tuple-element.213, s32[]{:T(128)} %get-tuple-element.203), kind=kOutput, calls=%fused_computation.6.clone.1 | convolution fusion | flops 807403520 | bytes 41975812 | tf_op jit(solution)/shard_map/while/body/eval_jaxpr/tijk,tijsuv->ksuv/dot_general | solution.py:140
  255.3 6.7 %constant_dynamic-slice_fusion.2 = bf16[1,4,2,4,128,4,128]{6,5,4,3,1,0,2:T(4,128)(2,1)} fusion(bf16[2,4,2,4,128,4,128]{6,5,4,3,1,0,2:T(4,128)(2,1)} %get-tuple-element.215, s32[]{:T(128)} %get-tuple-element.203), kind=kLoop, calls=%fused_computation.15.clone.1 | loop fusion | bytes 8388612 | tf_op jit(solution)/shard_map/while/body/jit(dynamic_index_in_dim)/dynamic_slice | solution.py:146
  262.0 7.5 %copy.392 = bf16[1,4,2,4,128,4,128]{4,6,2,1,5,3,0:T(8,128)(2,1)} copy(bf16[1,4,2,4,128,4,128]{6,5,4,3,1,0,2:T(4,128)(2,1)} %constant_dynamic-slice_fusion.2) | data formatting | bytes 8388608 | tf_op jit(solution)/shard_map/while/body/jit(dynamic_index_in_dim)/dynamic_slice | solution.py:146
  269.5 15.9 %convolution_bitcast_fusion.2 = f32[4,4,4,2,256,256]{4,5,3,0,2,1:T(8,128)} fusion(bf16[1,4,2,4,128,4,128]{4,6,2,1,5,3,0:T(8,128)(2,1)} %copy.392, bf16[2,4,4,256,128]{4,3,2,1,0:T(8,128)(2,1)} %get-tuple-element.216, s32[]{:T(128)} %get-tuple-element.203, bf16[2,4,4,256,128]{4,3,2,1,0:T(8,128)(2,1)S(1)} %get-tuple-element.214), kind=kOutput, calls=%fused_computation.2.clone.1 | convolution fusion | flops 3225419776 | bytes 39846912 | tf_op jit(solution)/shard_map/while/body/eval_jaxpr/tijsuy,ijvy->tijsuv/dot_general | solution.py:137
  285.4 39.9 %copy.393 = f32[4,4,4,2,256,256]{5,0,2,1,4,3:T(4,128)} copy(f32[4,4,4,2,256,256]{4,5,3,0,2,1:T(8,128)} %convolution_bitcast_fusion.2) | data formatting | bytes 67108864 | tf_op jit(solution)/shard_map/while/body/eval_jaxpr/tijsuy,ijvy->tijsuv/transpose | solution.py:137
  325.3 43.3 %bitcast_add_fusion.10 = f32[8,2,256,256]{3,0,2,1:T(8,128)} fusion(f32[8,2,256,256]{3,0,2,1:T(8,128)} %get-tuple-element.204, f32[4,4,4,2,256,256]{5,0,2,1,4,3:T(4,128)} %copy.393, pred[]{:T(512)S(6)} %compare.3, f32[2,4,4,4,8]{4,1,3,2,0:T(4,128)S(1)} %get-tuple-element.213, s32[]{:T(128)} %get-tuple-element.203), kind=kOutput, calls=%fused_computation.6.clone.1 | convolution fusion | flops 807403520 | bytes 41975812 | tf_op jit(solution)/shard_map/while/body/eval_jaxpr/tijk,tijsuv->ksuv/dot_general | solution.py:140
  368.5 5.6 copy.156
  374.2 176.7 %reduce-scatter.2.cloned.1.call-done = f32[128,256]{1,0:T(8,128)} async-done(((f32[4096,256]{1,0:T(8,128)}), f32[128,256]{1,0:T(8,128)}) %reduce-scatter.2.cloned.1.call-update) | async-done | bytes 131088 | tf_op jit(solution)/shard_map/reduce_scatter | solution.py:150
  550.9 56.8 %all-reduce.2.cloned.1.call-done = f32[128,256]{1,0:T(8,128)} async-done(((f32[128,256]{1,0:T(8,128)}), f32[128,256]{1,0:T(8,128)}) %all-reduce.2.cloned.1.call-update) | async-done | bytes 131088 | tf_op jit(solution)/shard_map/psum | solution.py:151
  (90 shorter events, 67.4 us)
Async XLA Ops:
  6.5 100.5 %copy-start = (bf16[8,256,128]{2,1,0:T(8,128)(2,1)S(1)}, bf16[8,256,128]{2,1,0:T(8,128)(2,1)}, u32[]{:S(2)}) copy-start(bf16[8,256,128]{2,1,0:T(8,128)(2,1)} %param.12) | copy-start | bytes 1572868
  6.5 544.4 %reduce-scatter.2.cloned.1.call-start = ((), (), s32[]{:S(2)}) async-start(), calls=%async_computation.1 | async-start | bytes 4325376 | tf_op jit(solution)/shard_map/reduce_scatter | solution.py:150
  14.2 7.6 %copy-start.3 = (f32[2,4,2,512]{3,2,1,0:T(2,128)S(1)}, f32[2,4,2,512]{3,2,1,0:T(2,128)}, u32[]{:S(2)}) copy-start(f32[2,4,2,512]{3,2,1,0:T(2,128)} %constant.27.clone.1) | copy-start | bytes 98308
  30.1 8.6 %slice-start = ((s8[8388608]{0:T(1024)(128)(4,1)}), s8[4194304]{0:T(1024)(128)(4,1)S(1)}, s32[]{:S(2)}) async-start(s8[8388608]{0:T(1024)(128)(4,1)} %bitcast.242), calls=%async_computation.3 | async-start | bytes 8388608
  34.5 4.1 slice-start.1
  94.4 12.2 %copy-start.6 = (s32[2]{0:T(128)S(1)}, s32[2]{0:T(128)}, u32[]{:S(2)}) copy-start(s32[2]{0:T(128)} %param.15) | copy-start | bytes 28
  94.4 12.3 %copy-start.5 = (s32[2,16]{1,0:T(2,128)S(1)}, s32[2,16]{1,0:T(2,128)}, u32[]{:S(2)}) copy-start(s32[2,16]{1,0:T(2,128)} %param.13) | copy-start | bytes 388
  94.4 12.4 %copy-start.4 = (s32[2,4,16]{2,1,0:T(4,128)S(1)}, s32[2,4,16]{2,1,0:T(4,128)}, u32[]{:S(2)}) copy-start(s32[2,4,16]{2,1,0:T(4,128)} %param.14) | copy-start | bytes 1540
  94.5 13.6 %copy-start.2 = (bf16[8,256,128]{2,1,0:T(8,128)(2,1)S(1)}, bf16[8,256,128]{2,1,0:T(8,128)(2,1)}, u32[]{:S(2)}) copy-start(bf16[8,256,128]{2,1,0:T(8,128)(2,1)} %param.11) | copy-start | bytes 1572868
  100.1 10.1 %collective-permute-start = (f32[2,2,2,512]{3,1,0,2:T(2,128)S(1)}, f32[2,2,2,512]{3,1,0,2:T(2,128)S(1)}, u32[]{:S(2)}, u32[]{:S(2)}) collective-permute-start(f32[2,2,2,512]{3,1,0,2:T(2,128)S(1)} %get-tuple-element.113), channel_id=1, source_target_pairs={{0,1},{1,2},{2,3},{4,5},{5,6},{6,7},{8,9},{9,10},{10,11},{12,13},{... | collective-permute-start | bytes 49160 | tf_op jit(solution)/shard_map/ppermute | solution.py:25
  104.6 5.6 collective-permute-start.1
  368.5 240.8 %copy-start.1 = (bf16[8,256,128]{2,1,0:T(8,128)(2,1)S(1)}, bf16[8,256,128]{2,1,0:T(8,128)(2,1)}, u32[]{:S(2)}) copy-start(bf16[8,256,128]{2,1,0:T(8,128)(2,1)} %param.12) | copy-start | bytes 1572868
  374.1 233.6 %all-reduce.2.cloned.1.call-start = ((), (), s32[]{:S(2)}) async-start(), calls=%async_computation.2 | async-start | bytes 262144 | tf_op jit(solution)/shard_map/psum | solution.py:151
Sparse Core Ops, SparseCore 0:
  374.2 176.6 reduce-scatter.1
  553.4 54.2 all-reduce.1
where the time goes:
time: 623 us; the launch traced here: 617 us
  waiting for transfers between devices  234 us (38%)
  matrix products  203 us (33%)
  local copies, waits for them, and re-layouts  133 us (21%)
  other arithmetic  26.5 us (4%)
  between operations  14.2 us (2%)
  starting transfers between devices  6.47 us (1%)
    reduce_scatter x1, waiting for transfers between devices, local(): lax.psum_scatter(bank_terms, 'chan', scatter_dimension=0, tiled=True)  177 us
    dot_general x2, matrix products, per_channel(): jnp.einsum('tijk,tijsuv->ksuv', hits_one, contrib, precision=lax.Precisio...  86.2 us
    dot_general x18, matrix products, contract_rows(): jnp.einsum('...kq,...qp->...kp', vectors, matrix, precision=lax.Precision...  84.8 us
    transpose x2, local copies, waits for them, and re-layouts, per_channel(): jnp.einsum('tijsuy,ijvy->tijsuv', formed, right_one, preferred_element_ty...  79.8 us
    psum x1, waiting for transfers between devices, local(): result = lax.psum(shares, 'tm')  56.8 us
    dot_general x2, matrix products, per_channel(): jnp.einsum('tijsuy,ijvy->tijsuv', formed, right_one, preferred_element_ty...  31.8 us
    dynamic_slice x4, local copies, waits for them, and re-layouts, local(): lax.scan(per_channel, start_banks, (pieces, left_groups, right_groups, ba...  28.4 us
    another operation x2, local copies, waits for them, and re-layouts, calibrate(): return jnp.stack([out_re, out_im], axis=-3).astype(jnp.bfloat16)  13.8 us
  transfers between devices with their start and end apart: 4, of which 2 were waited for; matrix products, arithmetic and copies ran while one was open for 1% of the time, Pallas kernels for 0%

commit v1 on v0

v1 whole, which is shorter than its diff:
```python
import jax
import jax.numpy as jnp
from jax import lax
from jax.experimental import pallas as pl
from jax.experimental.pallas import tpu as pltpu
from jax.sharding import PartitionSpec as P

N = 512
BLK = 128
BEAMS = 256
BANKS = 8
NWEIGHT = 8
ITERS = 6
HW = 2
LC = 2
LT = 4
TMS = 4
ALL_T = 16
MATS = LC * LT
MESH = pl.DeviceIdType.MESH
MIB = 1024 * 1024
F32 = jnp.float32
BF16 = jnp.bfloat16

epsilon = 1e-06


def split(x):
    high = x.astype(BF16).astype(F32)
    return high, x - high


def gains_kernel(vis_ref, mod_ref, out_ref, mats):
    step = pl.program_id(0)
    strip = 64
    for top in range(0, N, strip):
        rows = slice(top, top + strip)
        vis_re = vis_ref[0, 0, rows, :].astype(F32)
        vis_im = vis_ref[0, 1, rows, :].astype(F32)
        mod_re = mod_ref[0, 0, rows, :].astype(F32)
        mod_im = mod_ref[0, 1, rows, :].astype(F32)
        mats[step, 0, rows, :] = (mod_re * vis_re + mod_im * vis_im).astype(BF16)
        mats[step, 1, rows, :] = (mod_im * vis_re - mod_re * vis_im).astype(BF16)
        mats[step, 2, rows, :] = (mod_re * mod_re + mod_im * mod_im).astype(BF16)

    @pl.when(step == MATS - 1)
    def _():
        row = lax.broadcasted_iota(jnp.int32, (MATS, N), 0)

        def sweep(k, gains):
            gain_re, gain_im = gains
            power = gain_re * gain_re + gain_im * gain_im
            both = jnp.concatenate([*split(gain_re), *split(gain_im)], axis=0).astype(BF16)
            size = jnp.concatenate(split(power), axis=0).astype(BF16)
            num_re = jnp.zeros((MATS, N), F32)
            num_im = jnp.zeros((MATS, N), F32)
            den = jnp.zeros((MATS, N), F32)
            for m in range(MATS):
                with_re = jnp.dot(both, mats[m, 0], preferred_element_type=F32)
                with_im = jnp.dot(both, mats[m, 1], preferred_element_type=F32)
                with_pw = jnp.dot(size, mats[m, 2], preferred_element_type=F32)
                one_re = (with_re[0:8] + with_re[8:16]) - (with_im[16:24] + with_im[24:32])
                one_im = (with_im[0:8] + with_im[8:16]) + (with_re[16:24] + with_re[24:32])
                mine = row == m
                num_re = jnp.where(mine, one_re, num_re)
                num_im = jnp.where(mine, one_im, num_im)
                den = jnp.where(mine, with_pw[0:8] + with_pw[8:16], den)
            den = den + epsilon
            new_re = num_re / den
            new_im = num_im / den
            odd = lax.rem(k, 2) == 1
            gain_re = jnp.where(odd, 0.5 * (new_re + gain_re), new_re)
            gain_im = jnp.where(odd, 0.5 * (new_im + gain_im), new_im)
            return gain_re, gain_im

        start = (jnp.ones((MATS, N), F32), jnp.zeros((MATS, N), F32))
        gain_re, gain_im = lax.fori_loop(0, ITERS, sweep, start)
        first_re = gain_re[:, 0:1]
        first_im = gain_im[:, 0:1]
        divisor = jnp.maximum(jnp.sqrt(first_re * first_re + first_im * first_im), 1.0)
        unit_re = first_re / divisor
        unit_im = -first_im / divisor
        out_ref[0] = gain_re * unit_re - gain_im * unit_im
        out_ref[1] = gain_re * unit_im + gain_im * unit_re


def referenced_gains(vis, mod):
    block = pl.BlockSpec((1, 2, N, N), lambda m: (m, 0, 0, 0))
    return pl.pallas_call(
        gains_kernel,
        grid=(MATS,),
        in_specs=[block, block],
        out_specs=pl.BlockSpec((2, MATS, N), lambda m: (0, 0, 0)),
        out_shape=jax.ShapeDtypeStruct((2, MATS, N), F32),
        scratch_shapes=[pltpu.VMEM((MATS, 3, N, N), BF16)],
        compiler_params=pltpu.CompilerParams(vmem_limit_bytes=40 * MIB),
        name="gains",
    )(vis, mod)


def smooth_kernel(width_ref, ref_ref, out_ref, halo, send_sem, recv_sem):
    me = lax.axis_index("tm")
    chan = lax.axis_index("chan")
    right = (chan, lax.rem(me + 1, TMS))
    left = (chan, lax.rem(me + TMS - 1, TMS))
    barrier = pltpu.get_barrier_semaphore()
    for other in (left, right):
        pl.semaphore_signal(barrier, inc=1, device_id=other, device_id_type=MESH)
    pl.semaphore_wait(barrier, 2)
    copies = [
        pltpu.make_async_remote_copy(
            src_ref=ref_ref,
            dst_ref=halo.at[slot],
            send_sem=send_sem.at[slot],
            recv_sem=recv_sem.at[slot],
            device_id=other,
            device_id_type=MESH,
        )
        for slot, other in ((0, right), (1, left))
    ]
    for copy in copies:
        copy.start()
    row = lax.broadcasted_iota(jnp.int32, (MATS, N), 0)
    within = lax.rem(row, LT)
    interval = me * LT + within
    width = jnp.where(row < LT, width_ref[0], width_ref[1])
    for copy in copies:
        copy.wait()

    def moved(x, offset):
        return x if offset % MATS == 0 else jnp.concatenate([x[offset % MATS :], x[: offset % MATS]], axis=0)

    sums = []
    for part in range(2):
        here = ref_ref[part]
        before = halo[0, part]
        after = halo[1, part]
        total = jnp.zeros((MATS, N), F32)
        count = jnp.zeros((MATS, N), F32)
        for offset in range(-HW, HW + 1):
            value = moved(here, offset)
            if offset > 0:
                value = jnp.where(within + offset < LT, value, moved(after, offset - LT))
            if offset < 0:
                value = jnp.where(within + offset >= 0, value, moved(before, offset + LT))
            inside = (width >= abs(offset)) & (interval + offset >= 0) & (interval + offset < ALL_T)
            total = total + jnp.where(inside, value, 0.0)
            count = count + jnp.where(inside, 1.0, 0.0)
        sums.append(total / count)
    smooth_re, smooth_im = sums
    size = jnp.maximum(smooth_re * smooth_re + smooth_im * smooth_im, 1.0)
    out_ref[0] = smooth_re / size
    out_ref[1] = -smooth_im / size


def inverse_gains(referenced, widths):
    return pl.pallas_call(
        smooth_kernel,
        in_specs=[
            pl.BlockSpec(memory_space=pltpu.SMEM),
            pl.BlockSpec(memory_space=pltpu.VMEM),
        ],
        out_specs=pl.BlockSpec(memory_space=pltpu.VMEM),
        out_shape=jax.ShapeDtypeStruct((2, MATS, N), F32),
        scratch_shapes=[
            pltpu.VMEM((2, 2, MATS, N), F32),
            pltpu.SemaphoreType.DMA((2,)),
            pltpu.SemaphoreType.DMA((2,)),
        ],
        compiler_params=pltpu.CompilerParams(collective_id=0, has_side_effects=True),
        name="smooth",
    )(widths, referenced)


def sums_kernel(weight_ref, bank_ref, inv_ref, vis_ref, out_ref):
    step = pl.program_id(0)

    @pl.when(step == 0)
    def _():
        def clear(k, carry):
            out_ref[k] = jnp.zeros((BLK, 2 * BLK), F32)
            return carry

        lax.fori_loop(0, BANKS * NWEIGHT, clear, 0)

    re = inv_ref[0, pl.ds(step, 1), :]
    im = inv_ref[1, pl.ds(step, 1), :]
    re_high, re_low = split(re)
    im_high, im_low = split(im)
    row = lax.broadcasted_iota(jnp.int32, (16, N), 0)

    def stacked(rows):
        out = jnp.zeros((16, N), F32)
        for k, one in enumerate(rows):
            out = jnp.where(row == k, one, out)
        return out

    by_row_re = stacked([re_high, re_low, re_high, im_high, im_low, im_high]).astype(BF16)
    by_row_im = stacked([im_high, im_low, im_high, -re_high, -re_low, -re_high]).astype(BF16)
    by_col = stacked([re_high, re_high, re_low, im_high, im_high, im_low]).astype(BF16)
    depth_first = (((0,), (0,)), ((), ()))
    groups = N // BLK
    for i in range(groups):
        rows = slice(i * BLK, (i + 1) * BLK)
        scale_re = lax.dot_general(by_row_re[:, rows], by_col, depth_first, preferred_element_type=F32)
        scale_im = lax.dot_general(by_row_im[:, rows], by_col, depth_first, preferred_element_type=F32)
        for j in range(groups):
            cols = slice(j * BLK, (j + 1) * BLK)
            place = bank_ref[step, i * groups + j] * NWEIGHT + weight_ref[step // LT, i * groups + j]
            vis_re = vis_ref[0, 0, rows, cols].astype(F32)
            vis_im = vis_ref[0, 1, rows, cols].astype(F32)
            one_re = scale_re[:, cols]
            one_im = scale_im[:, cols]
            out_ref[place, :, 0:BLK] += one_re * vis_re - one_im * vis_im
            out_ref[place, :, BLK : 2 * BLK] += one_re * vis_im + one_im * vis_re


def calibrated_sums(weight_index, target_bank, inverse, vis):
    return pl.pallas_call(
        sums_kernel,
        grid=(MATS,),
        in_specs=[
            pl.BlockSpec(memory_space=pltpu.SMEM),
            pl.BlockSpec(memory_space=pltpu.SMEM),
            pl.BlockSpec((2, MATS, N), lambda m: (0, 0, 0)),
            pl.BlockSpec((1, 2, N, N), lambda m: (m, 0, 0, 0)),
        ],
        out_specs=pl.BlockSpec((BANKS * NWEIGHT, BLK, 2 * BLK), lambda m: (0, 0, 0)),
        out_shape=jax.ShapeDtypeStruct((BANKS * NWEIGHT, BLK, 2 * BLK), F32),
        compiler_params=pltpu.CompilerParams(vmem_limit_bytes=40 * MIB),
        name="sums",
    )(weight_index, target_bank, inverse, vis)


ORDERS = (("x", "y", "z"), ("y", "z", "x"), ("z", "x", "y"))
TILES = ((0, 3), (3, 6), (6, 8))
COUNTS = tuple(high - low for low, high in TILES)


def beams_kernel(left_ref, right_ref, sums_ref, out_ref, *scratch):
    (held, lefts, rights, formed, terms, pair) = scratch[0:6]
    parts = scratch[6:9]
    relays = scratch[9:12]
    firsts = scratch[12:15]
    owns1 = scratch[15:18]
    seconds = scratch[18:21]
    owns2 = scratch[21:24]
    thirds = scratch[24:27]
    share = scratch[27]
    (load_sem, s0, r0, s1, r1, s2, r2, s3, r3, s4, r4) = scratch[28:39]

    chan = lax.axis_index("chan")
    tm = lax.axis_index("tm")
    z = lax.div(chan, 8)
    y = lax.rem(lax.div(chan, 2), 4)
    x_low = lax.div(tm, 2)
    x = lax.rem(chan, 2) * 2 + x_low
    core = lax.rem(tm, 2)
    place = {"x": x, "y": y, "z": z}

    def device(at, which=core):
        return (
            (at["z"] * 4 + at["y"]) * 2 + lax.div(at["x"], 2),
            lax.rem(at["x"], 2) * 2 + which,
        )

    def along(axis, by):
        return device({**place, axis: lax.rem(place[axis] + by, 4)})

    twin = device(place, 1 - core)
    other_low = lax.div(x, 2) * 2 + (1 - x_low)
    side = device({**place, "x": other_low})
    cross = device({**place, "x": other_low}, 1 - core)

    barrier = pltpu.get_barrier_semaphore()
    partners = [twin, cross] + [along(axis, by) for axis in "xyz" for by in (1, 2, 3)]
    for other in partners:
        pl.semaphore_signal(barrier, inc=1, device_id=other, device_id_type=MESH)

    def load(k):
        rows = pl.ds(k * NWEIGHT, NWEIGHT)
        return pltpu.make_async_copy(sums_ref.at[rows], held.at[rows], load_sem.at[k])

    for k in range(BANKS):
        load(k).start()
    for w in range(NWEIGHT):
        lefts[w] = jnp.concatenate([left_ref[w], left_ref[w]], axis=1)
        rights[:, w * BLK : (w + 1) * BLK] = right_ref[w]
    pl.semaphore_wait(barrier, len(partners))

    def remote(src, dst, send, recv, to):
        return pltpu.make_async_remote_copy(
            src_ref=src, dst_ref=dst, send_sem=send, recv_sem=recv, device_id=to, device_id_type=MESH
        )

    def pair_copy(k):
        return remote(terms.at[k, 1 - core], pair.at[k], s0.at[k], r0.at[k], twin)

    def bank(k, carry):
        load(k).wait()
        for w in range(NWEIGHT):
            high, low = split(held[k * NWEIGHT + w])
            both = jnp.concatenate([high, low], axis=0).astype(BF16)
            one = jnp.dot(lefts[w], both, preferred_element_type=F32).astype(BF16)
            formed[0, :, w * BLK : (w + 1) * BLK] = one[:, 0:BLK]
            formed[1, :, w * BLK : (w + 1) * BLK] = one[:, BLK : 2 * BLK]
        for part in range(2):
            term = lax.dot_general(
                formed[part], rights[...], (((1,), (1,)), ((), ())), preferred_element_type=F32
            )
            for half in range(2):
                cut = term[:, half * BLK : (half + 1) * BLK].reshape((4, 2, 4, 8, BLK))
                for which in range(2):
                    terms[k, which, part, :, half * 4 : half * 4 + 4] = cut[:, which]
        pair_copy(k).start()
        return carry

    lax.fori_loop(0, BANKS, bank, 0)

    def add_pair(k, carry):
        pair_copy(k).wait_recv()
        bz = lax.div(k, 2)
        for part in range(2):
            by = lax.rem(k, 2) * 2 + part
            both = terms[k, core, part] + pair[k, part]
            parts[0][:, by, bz] = both[:, 0:3]
            parts[1][by, bz] = both[:, 3:6]
            parts[2][bz, :, by] = both[:, 6:8]
        return carry

    lax.fori_loop(0, BANKS, add_pair, 0)

    copies = []
    for o in range(3):
        axis = ORDERS[o][0]
        at = place[axis]
        plus, minus, opposite = (lax.rem(at + by, 4) for by in (1, 3, 2))
        to_plus, to_minus = along(axis, 1), along(axis, 3)
        low, high = slice(0, 2), slice(2, 4)
        part, relay, first = parts[o], relays[o], firsts[o]
        moves = (
            (part.at[opposite, low], relay.at[0], to_plus),
            (part.at[opposite, high], relay.at[1], to_minus),
            (part.at[plus, high], first.at[0, high], to_plus),
            (part.at[minus, low], first.at[1, low], to_minus),
            (part.at[plus, low], first.at[0, low], to_plus),
            (part.at[minus, high], first.at[1, high], to_minus),
        )
        copies.append([remote(src, dst, s1.at[o, n], r1.at[o, n], to) for n, (src, dst, to) in enumerate(moves)])
    for pick in ((0, 1), (2, 3)):
        for o in range(3):
            for n in pick:
                copies[o][n].start()
    for o in range(3):
        at = place[ORDERS[o][0]]
        plus, minus = lax.rem(at + 1, 4), lax.rem(at + 3, 4)
        copies[o][0].wait_recv()
        parts[o][plus, 0:2] += relays[o][0]
        copies[o][4].start()
        copies[o][1].wait_recv()
        parts[o][minus, 2:4] += relays[o][1]
        copies[o][5].start()

    def exchange(source, slots, axis, send, recv):
        at = place[axis]
        made = []
        for n, by in enumerate((1, 3, 2)):
            made.append(
                remote(source.at[lax.rem(at + by, 4)], slots.at[n], send.at[n], recv.at[n], along(axis, by))
            )
        for copy in made:
            copy.start()
        return made

    later = []
    for o in range(3):
        for n in range(2, 6):
            copies[o][n].wait_recv()
        owns1[o][...] = parts[o][place[ORDERS[o][0]]] + firsts[o][0] + firsts[o][1]
        later.append(exchange(owns1[o], seconds[o], ORDERS[o][1], s2.at[o], r2.at[o]))
    last = []
    for o in range(3):
        for copy in later[o]:
            copy.wait_recv()
        slots = seconds[o]
        owns2[o][...] = owns1[o][place[ORDERS[o][1]]] + slots[0] + slots[1] + slots[2]
        last.append(exchange(owns2[o], thirds[o], ORDERS[o][2], s3.at[o], r3.at[o]))
    for o in range(3):
        for copy in last[o]:
            copy.wait_recv()
        slots = thirds[o]
        share[tm, TILES[o][0] : TILES[o][1]] = owns2[o][place[ORDERS[o][2]]] + slots[0] + slots[1] + slots[2]

    gathers = [
        remote(share.at[tm], share.at[tm], s4.at[n], r4.at[n], to) for n, to in enumerate((twin, side, cross))
    ]
    for copy in gathers:
        copy.start()
    for k in range(BANKS):
        pair_copy(k).wait_send()
    for group in copies + later + last:
        for copy in group:
            copy.wait_send()
    for copy in gathers:
        copy.wait_recv()
    for t in range(TMS):
        for half in range(2):
            for r in range(4):
                rows = slice(t * 32 + r * 8, t * 32 + r * 8 + 8)
                out_ref[rows, half * BLK : (half + 1) * BLK] = share[t, half * 4 + r]
    for copy in gathers:
        copy.wait_send()


def beam_banks(left, right, sums):
    tile = (8, BLK)
    vmem = lambda *dims: pltpu.VMEM(dims + tile, F32)
    dma = lambda *dims: pltpu.SemaphoreType.DMA(dims)
    scratch = [
        pltpu.VMEM((BANKS * NWEIGHT, BLK, 2 * BLK), F32),
        pltpu.VMEM((NWEIGHT, BEAMS, 2 * BLK), BF16),
        pltpu.VMEM((BEAMS, NWEIGHT * BLK), BF16),
        pltpu.VMEM((2, BEAMS, NWEIGHT * BLK), BF16),
        vmem(BANKS, 2, 2, 4, 8),
        vmem(BANKS, 2, 4, 8),
    ]
    scratch += [vmem(4, 4, 4, n) for n in COUNTS]
    scratch += [vmem(2, 2, 4, n) for n in COUNTS]
    scratch += [vmem(2, 4, 4, n) for n in COUNTS]
    scratch += [vmem(4, 4, n) for n in COUNTS]
    scratch += [vmem(3, 4, n) for n in COUNTS]
    scratch += [vmem(4, n) for n in COUNTS]
    scratch += [vmem(3, n) for n in COUNTS]
    scratch += [vmem(TMS, 8)]
    scratch += [dma(BANKS), dma(BANKS), dma(BANKS), dma(3, 6), dma(3, 6)]
    scratch += [dma(3, 3), dma(3, 3), dma(3, 3), dma(3, 3), dma(3), dma(3)]
    return pl.pallas_call(
        beams_kernel,
        in_specs=[
            pl.BlockSpec(memory_space=pltpu.VMEM),
            pl.BlockSpec(memory_space=pltpu.VMEM),
            pl.BlockSpec(memory_space=pl.ANY),
        ],
        out_specs=pl.BlockSpec(memory_space=pltpu.VMEM),
        out_shape=jax.ShapeDtypeStruct((BLK, BEAMS), F32),
        scratch_shapes=scratch,
        compiler_params=pltpu.CompilerParams(
            collective_id=1, has_side_effects=True, vmem_limit_bytes=48 * MIB
        ),
        name="beams",
    )(left, right, sums)


def local(visibilities, model, beam_left, beam_right, weight_index, target_bank, widths):
    vis = visibilities.reshape((MATS, 2, N, N))
    mod = model.reshape((MATS, 2, N, N))
    referenced = referenced_gains(vis, mod)
    inverse = inverse_gains(referenced, widths)
    sums = calibrated_sums(weight_index, target_bank.reshape((MATS, 16)), inverse, vis)
    return beam_banks(beam_left, beam_right, sums)


def solution(mesh):
    return jax.shard_map(
        local,
        mesh=mesh,
        in_specs=(
            P("chan", "tm", None, None, None),
            P("chan", "tm", None, None, None),
            P(),
            P(),
            P("chan", None),
            P("chan", "tm", None),
            P("chan"),
        ),
        out_specs=P("chan", None),
        check_vma=False,
    )
```

time: 623 us -> 81.4 us (0.13)
  waiting for transfers between devices: 234 us -> 0 us
  matrix products: 203 us -> 0 us
  local copies, waits for them, and re-layouts: 133 us -> 8.65 us
  Pallas kernels: 0 us -> 72.2 us
  other arithmetic: 26.5 us -> 0 us
  between operations: 14.2 us -> 0.07 us
  starting transfers between devices: 6.47 us -> 0 us
    dot_general x22 -> x0, matrix products: 203 us -> none  [the longest x2 86.2 us: per_channel(): jnp.einsum('tijk,tijsuv->ksuv', hits_one, contrib, precision=lax.Precisio...]
    reduce_scatter x1 -> x0, waiting for transfers between devices: 177 us -> none  [local(): lax.psum_scatter(bank_terms, 'chan', scatter_dimension=0, tiled=True)]
    transpose x2 -> x0, local copies, waits for them, and re-layouts: 79.8 us -> none  [per_channel(): jnp.einsum('tijsuy,ijvy->tijsuv', formed, right_one, preferred_element_ty...]
    pallas_call x0 -> x4, Pallas kernels: none -> 72.2 us  [the longest x1 35 us: beam_banks(): pl.pallas_call(beams_kernel, in_specs=[pl.BlockSpec(memory_space=pltpu.VM...]
    psum x1 -> x0, waiting for transfers between devices: 56.8 us -> none  [local(): result = lax.psum(shares, 'tm')]
    dynamic_slice x4 -> x0, local copies, waits for them, and re-layouts: 28.4 us -> none  [local(): lax.scan(per_channel, start_banks, (pieces, left_groups, right_groups, ba...]
    another operation x13 -> x0, other arithmetic: 18.2 us -> none
    another operation x2 -> x0, local copies, waits for them, and re-layouts: 13.8 us -> none  [calibrate(): return jnp.stack([out_re, out_im], axis=-3).astype(jnp.bfloat16)]
  transfers between devices with their start and end apart: 4 -> 0, of which waited for: 2 -> 0; matrix products, arithmetic and copies ran while one was open for 1% -> 0% of each run, Pallas kernels for 0% -> 0%
where the time goes in v1:
time: 81.4 us; the launch traced here: 80.9 us
  Pallas kernels  72.2 us (89%)
  local copies, waits for them, and re-layouts  8.65 us (11%)
    pallas_call x1, Pallas kernels, beam_banks(): pl.pallas_call(beams_kernel, in_specs=[pl.BlockSpec(memory_space=pltpu.VM...  35 us
    pallas_call x1, Pallas kernels, referenced_gains(): pl.pallas_call(gains_kernel, grid=(MATS,), in_specs=[block, block], out_s...  20.8 us
    pallas_call x1, Pallas kernels, calibrated_sums(): pl.pallas_call(sums_kernel, grid=(MATS,), in_specs=[pl.BlockSpec(memory_s...  10.3 us
    unnamed x17, local copies, waits for them, and re-layouts  8.65 us
    pallas_call x1, Pallas kernels, inverse_gains(): pl.pallas_call(smooth_kernel, in_specs=[pl.BlockSpec(memory_space=pltpu.S...  6.04 us

profile of v1, /device:TPU:1, one launch (start us, length us, event | category | flops | bytes accessed | tf_op | source)
XLA Modules:
  0.0 80.9 jit_solution(13462859626641334989)
XLA Ops:
  0.0 0.0 copy-start.1
  0.0 3.4 %copy-done.1 = bf16[2,4,2,512,512]{4,3,2,1,0:T(8,128)(2,1)S(1)} copy-done((bf16[2,4,2,512,512]{4,3,2,1,0:T(8,128)(2,1)S(1)}, bf16[2,4,2,512,512]{4,3,2,1,0:T(8,128)(2,1)}, u32[]{:S(2)}) %copy-start.1) | copy-done | bytes 8388632
  3.4 0.0 copy-start.6
  3.4 0.0 copy-start.7
  3.4 20.8 %gains.1.ref_ref = f32[2,8,512]{2,1,0:T(8,128)S(1)} custom-call(bf16[8,2,512,512]{3,2,1,0:T(8,128)(2,1)S(1)} %bitcast.4, bf16[8,2,512,512]{3,2,1,0:T(8,128)(2,1)} %bitcast.6), custom_call_target="tpu_custom_call" | custom-call | tf_op jit(solution)/shard_map/gains/pallas_call | solution.py:89
  24.2 0.0 copy-start.5
  24.2 0.6 copy-done.5
  24.8 6.0 %smooth.1.inv_ref = f32[2,8,512]{2,1,0:T(8,128)} custom-call(s32[2]{0:T(128)} %width_ref.1, f32[2,8,512]{2,1,0:T(8,128)} %copy-done.5), custom_call_target="tpu_custom_call" | custom-call | tf_op jit(solution)/shard_map/smooth/pallas_call | solution.py:157
  30.9 0.0 copy-done.6
  30.9 0.0 copy-done.7
  30.9 0.0 copy-start.4
  30.9 0.7 copy-done.4
  31.6 0.0 copy-start.2
  31.6 0.0 copy-start.3
  31.6 10.3 %sums.1.sums_ref = f32[64,128,256]{2,1,0:T(8,128)S(1)} custom-call(s32[2,16]{1,0:T(2,128)S(1)} %copy-done.7, s32[8,16]{1,0:T(8,128)S(1)} %bitcast.5, f32[2,8,512]{2,1,0:T(8,128)S(1)} %copy-done.4, bf16[8,2,512,512]{3,2,1,0:T(8,128)(2,1)} %bitcast.3), custom_call_target="tpu_custom_call" | custom-call | tf_op jit(solution)/shard_map/sums/pallas_call | solution.py:219
  42.0 0.0 copy-start
  42.0 3.2 %copy-done = f32[64,128,256]{2,1,0:T(8,128)} copy-done((f32[64,128,256]{2,1,0:T(8,128)}, f32[64,128,256]{2,1,0:T(8,128)S(1)}, u32[]{:S(2)}) %copy-start) | copy-done | bytes 8388632
  45.2 0.0 copy-done.2
  45.2 0.0 copy-done.3
  45.2 35.0 %beams.1 = f32[128,256]{1,0:T(8,128)S(1)} custom-call(bf16[8,256,128]{2,1,0:T(8,128)(2,1)S(1)} %copy-done.2, bf16[8,256,128]{2,1,0:T(8,128)(2,1)S(1)} %copy-done.3, f32[64,128,256]{2,1,0:T(8,128)} %copy-done), custom_call_target="tpu_custom_call" | custom-call | tf_op jit(solution)/shard_map/beams/pallas_call | solution.py:437
  80.2 0.7 copy.9
Async XLA Ops:
  0.0 3.4 %copy-start.1 = (bf16[2,4,2,512,512]{4,3,2,1,0:T(8,128)(2,1)S(1)}, bf16[2,4,2,512,512]{4,3,2,1,0:T(8,128)(2,1)}, u32[]{:S(2)}) copy-start(bf16[2,4,2,512,512]{4,3,2,1,0:T(8,128)(2,1)} %param.7) | copy-start | bytes 25165828
  3.4 27.5 %copy-start.6 = (s32[2,4,16]{2,1,0:T(4,128)S(1)}, s32[2,4,16]{2,1,0:T(4,128)}, u32[]{:S(2)}) copy-start(s32[2,4,16]{2,1,0:T(4,128)} %param.12) | copy-start | bytes 1540
  3.4 27.5 %copy-start.7 = (s32[2,16]{1,0:T(2,128)S(1)}, s32[2,16]{1,0:T(2,128)}, u32[]{:S(2)}) copy-start(s32[2,16]{1,0:T(2,128)} %weight_ref.1) | copy-start | bytes 388
  24.2 0.6 copy-start.5
  30.9 0.8 copy-start.4
  31.6 13.6 %copy-start.2 = (bf16[8,256,128]{2,1,0:T(8,128)(2,1)S(1)}, bf16[8,256,128]{2,1,0:T(8,128)(2,1)}, u32[]{:S(2)}) copy-start(bf16[8,256,128]{2,1,0:T(8,128)(2,1)} %left_ref.1) | copy-start | bytes 1572868
  31.6 13.6 %copy-start.3 = (bf16[8,256,128]{2,1,0:T(8,128)(2,1)S(1)}, bf16[8,256,128]{2,1,0:T(8,128)(2,1)}, u32[]{:S(2)}) copy-start(bf16[8,256,128]{2,1,0:T(8,128)(2,1)} %right_ref.1) | copy-start | bytes 1572868
  42.0 3.2 %copy-start = (f32[64,128,256]{2,1,0:T(8,128)}, f32[64,128,256]{2,1,0:T(8,128)S(1)}, u32[]{:S(2)}) copy-start(f32[64,128,256]{2,1,0:T(8,128)S(1)} %sums.1.sums_ref) | copy-start | bytes 25165828

commit v2 on v1

v2 whole, which is shorter than its diff:
```python
import jax
import jax.numpy as jnp
from jax import lax
from jax.experimental import pallas as pl
from jax.experimental.pallas import tpu as pltpu
from jax.sharding import PartitionSpec as P

N = 512
BLK = 128
BEAMS = 256
BANKS = 8
NWEIGHT = 8
ITERS = 6
HW = 2
LC = 2
LT = 4
TMS = 4
ALL_T = 16
MATS = LC * LT
MESH = pl.DeviceIdType.MESH
MIB = 1024 * 1024
F32 = jnp.float32
BF16 = jnp.bfloat16

epsilon = 1e-06


def split(x):
    high = x.astype(BF16).astype(F32)
    return high, x - high


def gains_kernel(
    width_hbm, vis_hbm, mod_hbm, inv_ref, vis_ref,
    mod, cross, power, mine, halo, width, load_sem, width_sem, send_sem, recv_sem,
):
    me = lax.axis_index("tm")
    chan = lax.axis_index("chan")
    right = (chan, lax.rem(me + 1, TMS))
    left = (chan, lax.rem(me + TMS - 1, TMS))
    barrier = pltpu.get_barrier_semaphore()
    for other in (left, right):
        pl.semaphore_signal(barrier, inc=1, device_id=other, device_id_type=MESH)

    def load(m):
        return (
            pltpu.make_async_copy(vis_hbm.at[m], vis_ref.at[m], load_sem.at[0, m]),
            pltpu.make_async_copy(mod_hbm.at[m], mod.at[m], load_sem.at[1, m]),
        )

    for m in range(MATS):
        for copy in load(m):
            copy.start()
    width_copy = pltpu.make_async_copy(width_hbm, width, width_sem)
    width_copy.start()

    row = lax.broadcasted_iota(jnp.int32, (MATS, N), 0)
    strip = 32

    def form(m, sums):
        for copy in load(m):
            copy.wait()
        totals = [jnp.zeros((8, N), F32) for _ in range(3)]
        for top in range(0, N, strip):
            rows = slice(top, top + strip)
            vis_re = vis_ref[m, 0, rows, :].astype(F32)
            vis_im = vis_ref[m, 1, rows, :].astype(F32)
            mod_re = mod[m, 0, rows, :].astype(F32)
            mod_im = mod[m, 1, rows, :].astype(F32)
            cross_re = mod_re * vis_re + mod_im * vis_im
            cross_im = mod_im * vis_re - mod_re * vis_im
            size = mod_re * mod_re + mod_im * mod_im
            cross[m, 0, rows, :] = cross_re.astype(BF16)
            cross[m, 1, rows, :] = cross_im.astype(BF16)
            power[m, rows, :] = size
            for n, one in enumerate((cross_re, cross_im, size)):
                totals[n] = totals[n] + jnp.sum(one.reshape((strip // 8, 8, N)), axis=0)
        here = row == m
        return tuple(
            jnp.where(here, jnp.sum(total, axis=0, keepdims=True), old) for total, old in zip(totals, sums)
        )

    zeros = jnp.zeros((MATS, N), F32)
    num_re, num_im, den = lax.fori_loop(0, MATS, form, (zeros, zeros, zeros))
    den = den + epsilon

    def sweep(k, gains):
        gain_re, gain_im = gains
        size = gain_re * gain_re + gain_im * gain_im
        by_row = jnp.transpose(size)
        both = jnp.concatenate([*split(gain_re), *split(gain_im)], axis=0).astype(BF16)
        num_re, num_im, den = zeros, zeros, zeros
        for m in range(MATS):
            with_re = jnp.dot(both, cross[m, 0], preferred_element_type=F32)
            with_im = jnp.dot(both, cross[m, 1], preferred_element_type=F32)
            one_re = (with_re[0:8] + with_re[8:16]) - (with_im[16:24] + with_im[24:32])
            one_im = (with_im[0:8] + with_im[8:16]) + (with_re[16:24] + with_re[24:32])
            total = jnp.zeros((8, N), F32)
            for top in range(0, N, strip):
                rows = slice(top, top + strip)
                total = total + jnp.sum((by_row[rows, m : m + 1] * power[m, rows, :]).reshape((strip // 8, 8, N)), axis=0)
            here = row == m
            num_re = jnp.where(here, one_re, num_re)
            num_im = jnp.where(here, one_im, num_im)
            den = jnp.where(here, jnp.sum(total, axis=0, keepdims=True), den)
        den = den + epsilon
        new_re = num_re / den
        new_im = num_im / den
        odd = lax.rem(k, 2) == 1
        gain_re = jnp.where(odd, 0.5 * (new_re + gain_re), new_re)
        gain_im = jnp.where(odd, 0.5 * (new_im + gain_im), new_im)
        return gain_re, gain_im

    gain_re, gain_im = lax.fori_loop(1, ITERS, sweep, (num_re / den, num_im / den))
    first_re = gain_re[:, 0:1]
    first_im = gain_im[:, 0:1]
    divisor = jnp.maximum(jnp.sqrt(first_re * first_re + first_im * first_im), 1.0)
    unit_re = first_re / divisor
    unit_im = -first_im / divisor
    mine[0] = gain_re * unit_re - gain_im * unit_im
    mine[1] = gain_re * unit_im + gain_im * unit_re

    pl.semaphore_wait(barrier, 2)
    copies = [
        pltpu.make_async_remote_copy(
            src_ref=mine,
            dst_ref=halo.at[slot],
            send_sem=send_sem.at[slot],
            recv_sem=recv_sem.at[slot],
            device_id=other,
            device_id_type=MESH,
        )
        for slot, other in ((0, right), (1, left))
    ]
    for copy in copies:
        copy.start()
    width_copy.wait()
    within = lax.rem(row, LT)
    interval = me * LT + within
    half_width = jnp.where(row < LT, width[0], width[1])
    for copy in copies:
        copy.wait()

    def moved(x, offset):
        return x if offset % MATS == 0 else jnp.concatenate([x[offset % MATS :], x[: offset % MATS]], axis=0)

    sums = []
    for part in range(2):
        here = mine[part]
        before = halo[0, part]
        after = halo[1, part]
        total = jnp.zeros((MATS, N), F32)
        count = jnp.zeros((MATS, N), F32)
        for offset in range(-HW, HW + 1):
            value = moved(here, offset)
            if offset > 0:
                value = jnp.where(within + offset < LT, value, moved(after, offset - LT))
            if offset < 0:
                value = jnp.where(within + offset >= 0, value, moved(before, offset + LT))
            inside = (half_width >= abs(offset)) & (interval + offset >= 0) & (interval + offset < ALL_T)
            total = total + jnp.where(inside, value, 0.0)
            count = count + jnp.where(inside, 1.0, 0.0)
        sums.append(total / count)
    smooth_re, smooth_im = sums
    size = jnp.maximum(smooth_re * smooth_re + smooth_im * smooth_im, 1.0)
    inv_ref[0] = smooth_re / size
    inv_ref[1] = -smooth_im / size


def inverse_gains(widths, vis, mod):
    hbm = pl.BlockSpec(memory_space=pltpu.HBM)
    vmem = pl.BlockSpec(memory_space=pltpu.VMEM)
    return pl.pallas_call(
        gains_kernel,
        in_specs=[hbm, hbm, hbm],
        out_specs=[vmem, vmem],
        out_shape=[
            jax.ShapeDtypeStruct((2, MATS, N), F32),
            jax.ShapeDtypeStruct((MATS, 2, N, N), BF16),
        ],
        scratch_shapes=[
            pltpu.VMEM((MATS, 2, N, N), BF16),
            pltpu.VMEM((MATS, 2, N, N), BF16),
            pltpu.VMEM((MATS, N, N), F32),
            pltpu.VMEM((2, MATS, N), F32),
            pltpu.VMEM((2, 2, MATS, N), F32),
            pltpu.SMEM((LC,), jnp.int32),
            pltpu.SemaphoreType.DMA((2, MATS)),
            pltpu.SemaphoreType.DMA,
            pltpu.SemaphoreType.DMA((2,)),
            pltpu.SemaphoreType.DMA((2,)),
        ],
        compiler_params=pltpu.CompilerParams(
            collective_id=0, has_side_effects=True, vmem_limit_bytes=34 * MIB
        ),
        name="gains",
    )(*(pltpu.with_memory_space_constraint(x, pltpu.HBM) for x in (widths, vis, mod)))


def sums_kernel(weight_hbm, bank_hbm, inv_ref, vis_ref, out_ref, weight, bank, scale_a, scale_b, sem):
    copies = [
        pltpu.make_async_copy(weight_hbm, weight, sem.at[0]),
        pltpu.make_async_copy(bank_hbm, bank, sem.at[1]),
    ]
    for copy in copies:
        copy.start()
    row = lax.broadcasted_iota(jnp.int32, (16, N), 0)
    groups = N // BLK
    strip = 32

    def stacked(rows):
        out = jnp.zeros((16, N), F32)
        for k, one in enumerate(rows):
            out = jnp.where(row == k, one, out)
        return out.astype(BF16)

    def scales(m, scale):
        re_high, re_low = split(inv_ref[0, pl.ds(m, 1), :])
        im_high, im_low = split(inv_ref[1, pl.ds(m, 1), :])
        by_row_re = stacked([re_high, re_low, re_high, im_high, im_low, im_high])
        by_row_im = stacked([im_high, im_low, im_high, -re_high, -re_low, -re_high])
        by_col = stacked([re_high, re_high, re_low, im_high, im_high, im_low])
        depth_first = (((0,), (0,)), ((), ()))
        scale[0] = lax.dot_general(by_row_re, by_col, depth_first, preferred_element_type=F32)
        scale[1] = lax.dot_general(by_row_im, by_col, depth_first, preferred_element_type=F32)

    def add(m, c, scale):
        for i in range(groups):
            for j in range(groups):
                cols = slice(j * BLK, (j + 1) * BLK)
                place = bank[m, i * groups + j] * NWEIGHT + weight[c, i * groups + j]
                for s in range(0, BLK, strip):
                    rows = slice(i * BLK + s, i * BLK + s + strip)
                    to = slice(s, s + strip)
                    vis_re = vis_ref[m, 0, rows, cols].astype(F32)
                    vis_im = vis_ref[m, 1, rows, cols].astype(F32)
                    one_re = scale[0, rows, cols]
                    one_im = scale[1, rows, cols]
                    out_ref[place, to, 0:BLK] += one_re * vis_re - one_im * vis_im
                    out_ref[place, to, BLK : 2 * BLK] += one_re * vis_im + one_im * vis_re

    def clear(k, carry):
        out_ref[k] = jnp.zeros((BLK, 2 * BLK), F32)
        return carry

    scales(0, scale_a)
    lax.fori_loop(0, BANKS * NWEIGHT, clear, 0)
    for copy in copies:
        copy.wait()

    def two(q, carry):
        c = lax.div(q, LT // 2)
        scales(2 * q + 1, scale_b)
        add(2 * q, c, scale_a)
        scales(jnp.minimum(2 * q + 2, MATS - 1), scale_a)
        add(2 * q + 1, c, scale_b)
        return carry

    lax.fori_loop(0, MATS // 2, two, 0)


def calibrated_sums(weight_index, target_bank, inverse, vis):
    hbm = pl.BlockSpec(memory_space=pltpu.HBM)
    vmem = pl.BlockSpec(memory_space=pltpu.VMEM)
    return pl.pallas_call(
        sums_kernel,
        in_specs=[hbm, hbm, vmem, vmem],
        out_specs=vmem,
        out_shape=jax.ShapeDtypeStruct((BANKS * NWEIGHT, BLK, 2 * BLK), F32),
        scratch_shapes=[
            pltpu.SMEM((LC, 16), jnp.int32),
            pltpu.SMEM((MATS, 16), jnp.int32),
            pltpu.VMEM((2, N, N), F32),
            pltpu.VMEM((2, N, N), F32),
            pltpu.SemaphoreType.DMA((2,)),
        ],
        compiler_params=pltpu.CompilerParams(vmem_limit_bytes=12 * MIB),
        name="sums",
    )(*(pltpu.with_memory_space_constraint(x, pltpu.HBM) for x in (weight_index, target_bank)), inverse, vis)


ORDERS = (("x", "y", "z"), ("y", "z", "x"), ("z", "x", "y"))
TILES = ((0, 3), (3, 6), (6, 8))
COUNTS = tuple(high - low for low, high in TILES)


def beams_kernel(left_ref, right_ref, sums_ref, out_ref, *scratch):
    (lefts, rights, formed, terms, pair) = scratch[0:5]
    parts = scratch[5:8]
    relays = scratch[8:11]
    firsts = scratch[11:14]
    owns1 = scratch[14:17]
    seconds = scratch[17:20]
    owns2 = scratch[20:23]
    thirds = scratch[23:26]
    share = scratch[26]
    (s0, r0, s1, r1, s2, r2, s3, r3, s4, r4) = scratch[27:37]

    chan = lax.axis_index("chan")
    tm = lax.axis_index("tm")
    z = lax.div(chan, 8)
    y = lax.rem(lax.div(chan, 2), 4)
    x_low = lax.div(tm, 2)
    x = lax.rem(chan, 2) * 2 + x_low
    core = lax.rem(tm, 2)
    place = {"x": x, "y": y, "z": z}

    def device(at, which=core):
        return (
            (at["z"] * 4 + at["y"]) * 2 + lax.div(at["x"], 2),
            lax.rem(at["x"], 2) * 2 + which,
        )

    def along(axis, by):
        return device({**place, axis: lax.rem(place[axis] + by, 4)})

    twin = device(place, 1 - core)
    other_low = lax.div(x, 2) * 2 + (1 - x_low)
    side = device({**place, "x": other_low})
    cross = device({**place, "x": other_low}, 1 - core)

    barrier = pltpu.get_barrier_semaphore()
    partners = [twin, cross] + [along(axis, by) for axis in "xyz" for by in (1, 2, 3)]
    for other in partners:
        pl.semaphore_signal(barrier, inc=1, device_id=other, device_id_type=MESH)

    for w in range(NWEIGHT):
        lefts[w] = jnp.concatenate([left_ref[w], left_ref[w]], axis=1)
        rights[:, w * BLK : (w + 1) * BLK] = right_ref[w]
    pl.semaphore_wait(barrier, len(partners))

    def remote(src, dst, send, recv, to):
        return pltpu.make_async_remote_copy(
            src_ref=src, dst_ref=dst, send_sem=send, recv_sem=recv, device_id=to, device_id_type=MESH
        )

    def pair_copy(k):
        return remote(terms.at[k, 1 - core], pair.at[k], s0.at[k], r0.at[k], twin)

    def bank(k, carry):
        for w in range(NWEIGHT):
            high, low = split(sums_ref[k * NWEIGHT + w])
            both = jnp.concatenate([high, low], axis=0).astype(BF16)
            one = jnp.dot(lefts[w], both, preferred_element_type=F32).astype(BF16)
            formed[0, :, w * BLK : (w + 1) * BLK] = one[:, 0:BLK]
            formed[1, :, w * BLK : (w + 1) * BLK] = one[:, BLK : 2 * BLK]
        for part in range(2):
            term = lax.dot_general(
                formed[part], rights[...], (((1,), (1,)), ((), ())), preferred_element_type=F32
            )
            for half in range(2):
                cut = term[:, half * BLK : (half + 1) * BLK].reshape((4, 2, 4, 8, BLK))
                for which in range(2):
                    terms[k, which, part, :, half * 4 : half * 4 + 4] = cut[:, which]
        pair_copy(k).start()
        return carry

    lax.fori_loop(0, BANKS, bank, 0)

    def add_pair(k, carry):
        pair_copy(k).wait_recv()
        bz = lax.div(k, 2)
        for part in range(2):
            by = lax.rem(k, 2) * 2 + part
            both = terms[k, core, part] + pair[k, part]
            parts[0][:, by, bz] = both[:, 0:3]
            parts[1][by, bz] = both[:, 3:6]
            parts[2][bz, :, by] = both[:, 6:8]
        return carry

    lax.fori_loop(0, BANKS, add_pair, 0)

    copies = []
    for o in range(3):
        axis = ORDERS[o][0]
        at = place[axis]
        plus, minus, opposite = (lax.rem(at + by, 4) for by in (1, 3, 2))
        to_plus, to_minus = along(axis, 1), along(axis, 3)
        low, high = slice(0, 2), slice(2, 4)
        part, relay, first = parts[o], relays[o], firsts[o]
        moves = (
            (part.at[opposite, low], relay.at[0], to_plus),
            (part.at[opposite, high], relay.at[1], to_minus),
            (part.at[plus, high], first.at[0, high], to_plus),
            (part.at[minus, low], first.at[1, low], to_minus),
            (part.at[plus, low], first.at[0, low], to_plus),
            (part.at[minus, high], first.at[1, high], to_minus),
        )
        copies.append([remote(src, dst, s1.at[o, n], r1.at[o, n], to) for n, (src, dst, to) in enumerate(moves)])
    for pick in ((0, 1), (2, 3)):
        for o in range(3):
            for n in pick:
                copies[o][n].start()
    for o in range(3):
        at = place[ORDERS[o][0]]
        plus, minus = lax.rem(at + 1, 4), lax.rem(at + 3, 4)
        copies[o][0].wait_recv()
        parts[o][plus, 0:2] += relays[o][0]
        copies[o][4].start()
        copies[o][1].wait_recv()
        parts[o][minus, 2:4] += relays[o][1]
        copies[o][5].start()

    def exchange(source, slots, axis, send, recv):
        at = place[axis]
        made = []
        for n, by in enumerate((1, 3, 2)):
            made.append(
                remote(source.at[lax.rem(at + by, 4)], slots.at[n], send.at[n], recv.at[n], along(axis, by))
            )
        for copy in made:
            copy.start()
        return made

    later = []
    for o in range(3):
        for n in range(2, 6):
            copies[o][n].wait_recv()
        owns1[o][...] = parts[o][place[ORDERS[o][0]]] + firsts[o][0] + firsts[o][1]
        later.append(exchange(owns1[o], seconds[o], ORDERS[o][1], s2.at[o], r2.at[o]))
    last = []
    for o in range(3):
        for copy in later[o]:
            copy.wait_recv()
        slots = seconds[o]
        owns2[o][...] = owns1[o][place[ORDERS[o][1]]] + slots[0] + slots[1] + slots[2]
        last.append(exchange(owns2[o], thirds[o], ORDERS[o][2], s3.at[o], r3.at[o]))
    for o in range(3):
        for copy in last[o]:
            copy.wait_recv()
        slots = thirds[o]
        share[tm, TILES[o][0] : TILES[o][1]] = owns2[o][place[ORDERS[o][2]]] + slots[0] + slots[1] + slots[2]

    gathers = [
        remote(share.at[tm], share.at[tm], s4.at[n], r4.at[n], to) for n, to in enumerate((twin, side, cross))
    ]
    for copy in gathers:
        copy.start()
    for k in range(BANKS):
        pair_copy(k).wait_send()
    for group in copies + later + last:
        for copy in group:
            copy.wait_send()
    for copy in gathers:
        copy.wait_recv()
    for t in range(TMS):
        for half in range(2):
            for r in range(4):
                rows = slice(t * 32 + r * 8, t * 32 + r * 8 + 8)
                out_ref[rows, half * BLK : (half + 1) * BLK] = share[t, half * 4 + r]
    for copy in gathers:
        copy.wait_send()


def beam_banks(left, right, sums):
    tile = (8, BLK)
    vmem = lambda *dims: pltpu.VMEM(dims + tile, F32)
    dma = lambda *dims: pltpu.SemaphoreType.DMA(dims)
    scratch = [
        pltpu.VMEM((NWEIGHT, BEAMS, 2 * BLK), BF16),
        pltpu.VMEM((BEAMS, NWEIGHT * BLK), BF16),
        pltpu.VMEM((2, BEAMS, NWEIGHT * BLK), BF16),
        vmem(BANKS, 2, 2, 4, 8),
        vmem(BANKS, 2, 4, 8),
    ]
    scratch += [vmem(4, 4, 4, n) for n in COUNTS]
    scratch += [vmem(2, 2, 4, n) for n in COUNTS]
    scratch += [vmem(2, 4, 4, n) for n in COUNTS]
    scratch += [vmem(4, 4, n) for n in COUNTS]
    scratch += [vmem(3, 4, n) for n in COUNTS]
    scratch += [vmem(4, n) for n in COUNTS]
    scratch += [vmem(3, n) for n in COUNTS]
    scratch += [vmem(TMS, 8)]
    scratch += [dma(BANKS), dma(BANKS), dma(3, 6), dma(3, 6)]
    scratch += [dma(3, 3), dma(3, 3), dma(3, 3), dma(3, 3), dma(3), dma(3)]
    return pl.pallas_call(
        beams_kernel,
        in_specs=[
            pl.BlockSpec(memory_space=pltpu.VMEM),
            pl.BlockSpec(memory_space=pltpu.VMEM),
            pl.BlockSpec(memory_space=pltpu.VMEM),
        ],
        out_specs=pl.BlockSpec(memory_space=pltpu.VMEM),
        out_shape=jax.ShapeDtypeStruct((BLK, BEAMS), F32),
        scratch_shapes=scratch,
        compiler_params=pltpu.CompilerParams(
            collective_id=1, has_side_effects=True, vmem_limit_bytes=24 * MIB
        ),
        name="beams",
    )(left, right, sums)


def local(visibilities, model, beam_left, beam_right, weight_index, target_bank, widths):
    vis = visibilities.reshape((MATS, 2, N, N))
    mod = model.reshape((MATS, 2, N, N))
    inverse, vis = inverse_gains(widths, vis, mod)
    sums = calibrated_sums(weight_index, target_bank.reshape((MATS, 16)), inverse, vis)
    return beam_banks(beam_left, beam_right, sums)


def solution(mesh):
    return jax.shard_map(
        local,
        mesh=mesh,
        in_specs=(
            P("chan", "tm", None, None, None),
            P("chan", "tm", None, None, None),
            P(),
            P(),
            P("chan", None),
            P("chan", "tm", None),
            P("chan"),
        ),
        out_specs=P("chan", None),
        check_vma=False,
    )
```

time: 81.4 us -> 62.4 us (0.77)
  Pallas kernels: 72.2 us -> 61.5 us
  local copies, waits for them, and re-layouts: 8.65 us -> 0.67 us
    pallas_call x3 -> x2, Pallas kernels: 37.1 us -> 27.2 us  [the longest x1 20.1 us: inverse_gains(): pl.pallas_call(gains_kernel, in_specs=[hbm, hbm, hbm], out_specs=[vmem, v...]
    unnamed x17 -> x5, local copies, waits for them, and re-layouts: 8.65 us -> 0.67 us
where the time goes in v2:
time: 62.4 us; the launch traced here: 62.3 us
  Pallas kernels  61.5 us (99%)
  local copies, waits for them, and re-layouts  0.67 us (1%)
    pallas_call x1, Pallas kernels, beam_banks(): pl.pallas_call(beams_kernel, in_specs=[pl.BlockSpec(memory_space=pltpu.VM...  34.3 us
    pallas_call x1, Pallas kernels, inverse_gains(): pl.pallas_call(gains_kernel, in_specs=[hbm, hbm, hbm], out_specs=[vmem, v...  20.1 us
    pallas_call x1, Pallas kernels, calibrated_sums(): pl.pallas_call(sums_kernel, in_specs=[hbm, hbm, vmem, vmem], out_specs=vm...  7.14 us

profile of v2, /device:TPU:1, one launch (start us, length us, event | category | flops | bytes accessed | tf_op | source)
XLA Modules:
  0.0 62.3 jit_solution(15227974119223329059)
XLA Ops:
  0.0 20.1 %gains.1 = (f32[2,8,512]{2,1,0:T(8,128)S(1)}, bf16[8,2,512,512]{3,2,1,0:T(8,128)(2,1)S(1)}) custom-call(s32[2]{0:T(128)} %width_hbm.1, bf16[8,2,512,512]{3,2,1,0:T(8,128)(2,1)} %bitcast.3, bf16[8,2,512,512]{3,2,1,0:T(8,128)(2,1)} %bitcast.4), custom_call_target="tpu_custom_call" | custom-call | tf_op jit(solution)/shard_map/gains/pallas_call | solution.py:173
  20.1 0.0 copy-start
  20.1 0.0 copy-start.1
  20.1 7.1 %sums.1.sums_ref = f32[64,128,256]{2,1,0:T(8,128)S(1)} custom-call(s32[2,16]{1,0:T(2,128)} %weight_hbm.1, s32[8,16]{1,0:T(8,128)} %bitcast.5, f32[2,8,512]{2,1,0:T(8,128)S(1)} %get-tuple-element.7.inv_ref, bf16[8,2,512,512]{3,2,1,0:T(8,128)(2,1)S(1)} %get-tuple-element.8.vis_ref), custom_call_target="tpu_custom_call" | custom-call | tf_op jit(solution)/shard_map/sums/pallas_call | solution.py:265
  27.2 0.0 copy-done
  27.3 0.0 copy-done.1
  27.3 34.3 %beams.1 = f32[128,256]{1,0:T(8,128)S(1)} custom-call(bf16[8,256,128]{2,1,0:T(8,128)(2,1)S(1)} %copy-done, bf16[8,256,128]{2,1,0:T(8,128)(2,1)S(1)} %copy-done.1, f32[64,128,256]{2,1,0:T(8,128)S(1)} %sums.1.sums_ref), custom_call_target="tpu_custom_call" | custom-call | tf_op jit(solution)/shard_map/beams/pallas_call | solution.py:476
  61.6 0.7 %copy.9 = f32[128,256]{1,0:T(8,128)} copy(f32[128,256]{1,0:T(8,128)S(1)} %beams.1) | data formatting | bytes 262144
Async XLA Ops:
  20.1 7.2 %copy-start = (bf16[8,256,128]{2,1,0:T(8,128)(2,1)S(1)}, bf16[8,256,128]{2,1,0:T(8,128)(2,1)}, u32[]{:S(2)}) copy-start(bf16[8,256,128]{2,1,0:T(8,128)(2,1)} %left_ref.1) | copy-start | bytes 1572868
  20.1 7.2 %copy-start.1 = (bf16[8,256,128]{2,1,0:T(8,128)(2,1)S(1)}, bf16[8,256,128]{2,1,0:T(8,128)(2,1)}, u32[]{:S(2)}) copy-start(bf16[8,256,128]{2,1,0:T(8,128)(2,1)} %right_ref.1) | copy-start | bytes 1572868

commit v3 on v2

v3 whole, which is shorter than its diff:
```python
import functools

import jax
import jax.numpy as jnp
from jax import lax
from jax.experimental import pallas as pl
from jax.experimental.pallas import tpu as pltpu
from jax.sharding import PartitionSpec as P

N = 512
BLK = 128
BEAMS = 256
BANKS = 8
NWEIGHT = 8
ITERS = 6
HW = 2
LC = 2
LT = 4
TMS = 4
ALL_T = 16
MATS = LC * LT
MESH = pl.DeviceIdType.MESH
MIB = 1024 * 1024
F32 = jnp.float32
BF16 = jnp.bfloat16

epsilon = 1e-06


def split(x):
    high = x.astype(BF16).astype(F32)
    return high, x - high


def gains_kernel(
    width_hbm, vis_hbm, mod_hbm, inv_ref, vis_ref,
    mod, cross_0, cross_1, power_0, power_1, sums_1, mine, halo, width, load_sem, width_sem, send_sem, recv_sem,
):
    me = lax.axis_index("tm")
    chan = lax.axis_index("chan")
    right = (chan, lax.rem(me + 1, TMS))
    left = (chan, lax.rem(me + TMS - 1, TMS))
    barrier = pltpu.get_barrier_semaphore()
    for other in (left, right):
        pl.semaphore_signal(barrier, inc=1, device_id=other, device_id_type=MESH)

    def load(m):
        return (
            pltpu.make_async_copy(vis_hbm.at[m], vis_ref.at[m], load_sem.at[0, m]),
            pltpu.make_async_copy(mod_hbm.at[m], mod.at[m], load_sem.at[1, m]),
        )

    for m in range(MATS):
        for copy in load(m):
            copy.start()
    width_copy = pltpu.make_async_copy(width_hbm, width, width_sem)
    width_copy.start()

    row = lax.broadcasted_iota(jnp.int32, (MATS, N), 0)
    zeros = jnp.zeros((MATS, N), F32)
    strip = 32
    strips = N // strip

    def form(m, slot, top, cross, power):
        rows = pl.ds(top, strip)
        vis_re = vis_ref[m, 0, rows, :].astype(F32)
        vis_im = vis_ref[m, 1, rows, :].astype(F32)
        mod_re = mod[m, 0, rows, :].astype(F32)
        mod_im = mod[m, 1, rows, :].astype(F32)
        cross_re = mod_re * vis_re + mod_im * vis_im
        cross_im = mod_im * vis_re - mod_re * vis_im
        size = mod_re * mod_re + mod_im * mod_im
        cross[slot, 0, rows, :] = cross_re.astype(BF16)
        cross[slot, 1, rows, :] = cross_im.astype(BF16)
        power[slot, rows, :] = size
        return [jnp.sum(one.reshape((strip // 8, 8, N)), axis=0) for one in (cross_re, cross_im, size)]

    def spread(totals, sums, m):
        here = row == m
        return tuple(
            jnp.where(here, jnp.sum(total, axis=0, keepdims=True), old) for total, old in zip(totals, sums)
        )

    def form_whole(m, sums):
        for copy in load(m):
            copy.wait()
        totals = [jnp.zeros((8, N), F32) for _ in range(3)]
        for top in range(0, N, strip):
            totals = [old + new for old, new in zip(totals, form(m, m, top, cross_0, power_0))]
        return spread(totals, sums, m)

    def sweep(k, gains, first, cross, power):
        gain_re, gain_im = gains
        size = gain_re * gain_re + gain_im * gain_im
        by_row = jnp.transpose(size)
        both = jnp.concatenate([*split(gain_re), *split(gain_im)], axis=0).astype(BF16)
        num_re, num_im, den = zeros, zeros, zeros
        for m in range(LT):
            with_re = jnp.dot(both, cross[m, 0], preferred_element_type=F32)
            with_im = jnp.dot(both, cross[m, 1], preferred_element_type=F32)
            one_re = (with_re[0:8] + with_re[8:16]) - (with_im[16:24] + with_im[24:32])
            one_im = (with_im[0:8] + with_im[8:16]) + (with_re[16:24] + with_re[24:32])
            total = jnp.zeros((8, N), F32)
            for top in range(0, N, strip):
                rows = slice(top, top + strip)
                by = by_row[rows, first + m : first + m + 1]
                total = total + jnp.sum((by * power[m, rows, :]).reshape((strip // 8, 8, N)), axis=0)
            here = row == first + m
            num_re = jnp.where(here, one_re, num_re)
            num_im = jnp.where(here, one_im, num_im)
            den = jnp.where(here, jnp.sum(total, axis=0, keepdims=True), den)
        den = den + epsilon
        new_re = num_re / den
        new_im = num_im / den
        odd = lax.rem(k, 2) == 1
        new_re = jnp.where(odd, 0.5 * (new_re + gain_re), new_re)
        new_im = jnp.where(odd, 0.5 * (new_im + gain_im), new_im)
        mine = (row >= first) & (row < first + LT)
        return jnp.where(mine, new_re, gain_re), jnp.where(mine, new_im, gain_im)

    num_re, num_im, den = lax.fori_loop(0, LT, form_whole, (zeros, zeros, zeros))
    den = den + epsilon
    sums_1[...] = jnp.zeros_like(sums_1)
    units = -(-LT * strips // (ITERS - 1))

    def beside(k, gains):
        @pl.when(k <= LT)
        def _():
            for copy in load(LT + k - 1):
                copy.wait()

        new = sweep(k, gains, 0, cross_0, power_0)
        for i in range(units):
            unit = (k - 1) * units + i
            real = unit < LT * strips
            unit = jnp.minimum(unit, LT * strips - 1)
            slot = lax.div(unit, strips)
            top = pl.multiple_of(lax.rem(unit, strips) * strip, strip)
            for n, total in enumerate(form(LT + slot, slot, top, cross_1, power_1)):
                sums_1[slot, n] += jnp.where(real, total, 0.0)
        return new

    gains = lax.fori_loop(1, ITERS, beside, (num_re / den, num_im / den))
    sums = (zeros, zeros, zeros)
    for m in range(LT):
        sums = spread([sums_1[m, n] for n in range(3)], sums, LT + m)
    num_re, num_im, den = sums
    den = den + epsilon
    later = row >= LT
    gains = (jnp.where(later, num_re / den, gains[0]), jnp.where(later, num_im / den, gains[1]))
    gain_re, gain_im = lax.fori_loop(1, ITERS, lambda k, gains: sweep(k, gains, LT, cross_1, power_1), gains)
    first_re = gain_re[:, 0:1]
    first_im = gain_im[:, 0:1]
    divisor = jnp.maximum(jnp.sqrt(first_re * first_re + first_im * first_im), 1.0)
    unit_re = first_re / divisor
    unit_im = -first_im / divisor
    mine[0] = gain_re * unit_re - gain_im * unit_im
    mine[1] = gain_re * unit_im + gain_im * unit_re

    pl.semaphore_wait(barrier, 2)
    copies = [
        pltpu.make_async_remote_copy(
            src_ref=mine,
            dst_ref=halo.at[slot],
            send_sem=send_sem.at[slot],
            recv_sem=recv_sem.at[slot],
            device_id=other,
            device_id_type=MESH,
        )
        for slot, other in ((0, right), (1, left))
    ]
    for copy in copies:
        copy.start()
    width_copy.wait()
    within = lax.rem(row, LT)
    interval = me * LT + within
    half_width = jnp.where(row < LT, width[0], width[1])
    for copy in copies:
        copy.wait()

    def moved(x, offset):
        return x if offset % MATS == 0 else jnp.concatenate([x[offset % MATS :], x[: offset % MATS]], axis=0)

    sums = []
    for part in range(2):
        here = mine[part]
        before = halo[0, part]
        after = halo[1, part]
        total = jnp.zeros((MATS, N), F32)
        count = jnp.zeros((MATS, N), F32)
        for offset in range(-HW, HW + 1):
            value = moved(here, offset)
            if offset > 0:
                value = jnp.where(within + offset < LT, value, moved(after, offset - LT))
            if offset < 0:
                value = jnp.where(within + offset >= 0, value, moved(before, offset + LT))
            inside = (half_width >= abs(offset)) & (interval + offset >= 0) & (interval + offset < ALL_T)
            total = total + jnp.where(inside, value, 0.0)
            count = count + jnp.where(inside, 1.0, 0.0)
        sums.append(total / count)
    smooth_re, smooth_im = sums
    size = jnp.maximum(smooth_re * smooth_re + smooth_im * smooth_im, 1.0)
    inv_ref[0] = smooth_re / size
    inv_ref[1] = -smooth_im / size


def inverse_gains(widths, vis, mod):
    hbm = pl.BlockSpec(memory_space=pltpu.HBM)
    vmem = pl.BlockSpec(memory_space=pltpu.VMEM)
    return pl.pallas_call(
        gains_kernel,
        in_specs=[hbm, hbm, hbm],
        out_specs=[vmem, vmem],
        out_shape=[
            jax.ShapeDtypeStruct((2, MATS, N), F32),
            jax.ShapeDtypeStruct((MATS, 2, N, N), BF16),
        ],
        scratch_shapes=[
            pltpu.VMEM((MATS, 2, N, N), BF16),
            pltpu.VMEM((LT, 2, N, N), BF16),
            pltpu.VMEM((LT, 2, N, N), BF16),
            pltpu.VMEM((LT, N, N), F32),
            pltpu.VMEM((LT, N, N), F32),
            pltpu.VMEM((LT, 3, 8, N), F32),
            pltpu.VMEM((2, MATS, N), F32),
            pltpu.VMEM((2, 2, MATS, N), F32),
            pltpu.SMEM((LC,), jnp.int32),
            pltpu.SemaphoreType.DMA((2, MATS)),
            pltpu.SemaphoreType.DMA,
            pltpu.SemaphoreType.DMA((2,)),
            pltpu.SemaphoreType.DMA((2,)),
        ],
        compiler_params=pltpu.CompilerParams(
            collective_id=0, has_side_effects=True, vmem_limit_bytes=34 * MIB
        ),
        name="gains",
    )(*(pltpu.with_memory_space_constraint(x, pltpu.HBM) for x in (widths, vis, mod)))


def sums_kernel(weight_hbm, bank_hbm, inv_ref, vis_ref, out_ref, weight, bank, row_a, row_b, col_a, col_b, sem):
    copies = [
        pltpu.make_async_copy(weight_hbm, weight, sem.at[0]),
        pltpu.make_async_copy(bank_hbm, bank, sem.at[1]),
    ]
    for copy in copies:
        copy.start()
    row = lax.broadcasted_iota(jnp.int32, (16, N), 0)
    groups = N // BLK
    strip = 32

    def stacked(rows):
        out = jnp.zeros((16, N), F32)
        for k, one in enumerate(rows):
            out = jnp.where(row == k, one, out)
        return out

    def factors(m, by_row, by_col):
        re_high, re_low = split(inv_ref[0, pl.ds(m, 1), :])
        im_high, im_low = split(inv_ref[1, pl.ds(m, 1), :])
        by_row[...] = jnp.transpose(stacked([re_high, re_low, re_high, im_high, im_low, im_high])).astype(BF16)
        col_re = stacked([re_high, re_high, re_low, im_high, im_high, im_low]).astype(BF16)
        col_im = stacked([-im_high, -im_high, -im_low, re_high, re_high, re_low]).astype(BF16)
        for j in range(groups):
            cols = slice(j * BLK, (j + 1) * BLK)
            by_col[j, :, 0:BLK] = col_re[:, cols]
            by_col[j, :, BLK : 2 * BLK] = col_im[:, cols]

    def add(m, c, by_row, by_col):
        for j in range(groups):
            cols = slice(j * BLK, (j + 1) * BLK)
            for i in range(groups):
                place = bank[m, i * groups + j] * NWEIGHT + weight[c, i * groups + j]
                scale = jnp.dot(by_row[i * BLK : (i + 1) * BLK, :], by_col[j], preferred_element_type=F32)
                for s in range(0, BLK, strip):
                    rows = slice(i * BLK + s, i * BLK + s + strip)
                    to = slice(s, s + strip)
                    vis_re = vis_ref[m, 0, rows, cols].astype(F32)
                    vis_im = vis_ref[m, 1, rows, cols].astype(F32)
                    one_re = scale[to, 0:BLK]
                    one_im = scale[to, BLK : 2 * BLK]
                    out_ref[place, to, 0:BLK] += one_re * vis_re - one_im * vis_im
                    out_ref[place, to, BLK : 2 * BLK] += one_re * vis_im + one_im * vis_re

    def clear(k, carry):
        out_ref[k] = jnp.zeros((BLK, 2 * BLK), F32)
        return carry

    factors(0, row_a, col_a)
    lax.fori_loop(0, BANKS * NWEIGHT, clear, 0)
    for copy in copies:
        copy.wait()

    def two(q, carry):
        c = lax.div(q, LT // 2)
        factors(2 * q + 1, row_b, col_b)
        add(2 * q, c, row_a, col_a)
        factors(jnp.minimum(2 * q + 2, MATS - 1), row_a, col_a)
        add(2 * q + 1, c, row_b, col_b)
        return carry

    lax.fori_loop(0, MATS // 2, two, 0)


def calibrated_sums(weight_index, target_bank, inverse, vis):
    hbm = pl.BlockSpec(memory_space=pltpu.HBM)
    vmem = pl.BlockSpec(memory_space=pltpu.VMEM)
    return pl.pallas_call(
        sums_kernel,
        in_specs=[hbm, hbm, vmem, vmem],
        out_specs=vmem,
        out_shape=jax.ShapeDtypeStruct((BANKS * NWEIGHT, BLK, 2 * BLK), F32),
        scratch_shapes=[
            pltpu.SMEM((LC, 16), jnp.int32),
            pltpu.SMEM((MATS, 16), jnp.int32),
            pltpu.VMEM((N, 16), BF16),
            pltpu.VMEM((N, 16), BF16),
            pltpu.VMEM((N // BLK, 16, 2 * BLK), BF16),
            pltpu.VMEM((N // BLK, 16, 2 * BLK), BF16),
            pltpu.SemaphoreType.DMA((2,)),
        ],
        compiler_params=pltpu.CompilerParams(vmem_limit_bytes=12 * MIB),
        name="sums",
    )(*(pltpu.with_memory_space_constraint(x, pltpu.HBM) for x in (weight_index, target_bank)), inverse, vis)


STEPS = (2, 1, 3, 0)
A, B, C = slice(0, 3), slice(3, 6), slice(6, 8)


def beams_kernel(left_ref, right_ref, sums_ref, out_ref, *scratch):
    (lefts, rights, formed, terms, pair) = scratch[0:5]
    (parts_a, first_a, own1_a, second_a, own2_a, last_a) = scratch[5:11]
    (parts_b, first_b, own1_b, second_b, own2_b, last_b) = scratch[11:17]
    (parts_c, first_c, own1_c, second_c, own2_c, last_c) = scratch[17:23]
    share = scratch[23]
    sems = scratch[24:]
    (s_pair, s_a1, s_a2, s_a3, s_b1, s_b2, s_b3, s_c1, s_c2, s_c3, s_all) = sems[0:11]
    (r_pair, r_a1, r_a2, r_a3, r_b1, r_b2, r_b3, r_c1, r_c2, r_c3, r_all) = sems[11:22]

    chan = lax.axis_index("chan")
    tm = lax.axis_index("tm")
    z = lax.div(chan, 8)
    y = lax.rem(lax.div(chan, 2), 4)
    x_low = lax.div(tm, 2)
    x = lax.rem(chan, 2) * 2 + x_low
    core = lax.rem(tm, 2)
    place = {"x": x, "y": y, "z": z}

    def device(at, which=core):
        return (
            (at["z"] * 4 + at["y"]) * 2 + lax.div(at["x"], 2),
            lax.rem(at["x"], 2) * 2 + which,
        )

    def at(axis, by):
        return lax.rem(place[axis] + by, 4)

    near = {(axis, by): device({**place, axis: at(axis, by)}) for axis in "xyz" for by in (1, 2, 3)}
    twin = device(place, 1 - core)
    other_low = lax.div(x, 2) * 2 + (1 - x_low)
    side = device({**place, "x": other_low})
    cross = device({**place, "x": other_low}, 1 - core)

    barrier = pltpu.get_barrier_semaphore()
    partners = [twin, cross, *near.values()]
    for other in partners:
        pl.semaphore_signal(barrier, inc=1, device_id=other, device_id_type=MESH)

    for w in range(NWEIGHT):
        lefts[w] = jnp.concatenate([left_ref[w], left_ref[w]], axis=1)
        rights[:, w * BLK : (w + 1) * BLK] = right_ref[w]

    def remote(src, dst, send, recv, to):
        return pltpu.make_async_remote_copy(
            src_ref=src, dst_ref=dst, send_sem=send, recv_sem=recv, device_id=to, device_id_type=MESH
        )

    started = []

    def go(copies):
        for copy in copies:
            copy.start()
        started.extend(copies)

    def pair_copy(n):
        return remote(terms.at[n, 1 - core], pair.at[n], s_pair.at[n], r_pair.at[n], twin)

    def bank(n, step):
        k = at("z", STEPS[step]) * 2 + lax.rem(n, 2)
        for w in range(NWEIGHT):
            high, low = split(sums_ref[k * NWEIGHT + w])
            both = jnp.concatenate([high, low], axis=0).astype(BF16)
            one = jnp.dot(lefts[w], both, preferred_element_type=F32).astype(BF16)
            formed[0, :, w * BLK : (w + 1) * BLK] = one[:, 0:BLK]
            formed[1, :, w * BLK : (w + 1) * BLK] = one[:, BLK : 2 * BLK]
        for part in range(2):
            term = lax.dot_general(
                formed[part], rights[...], (((1,), (1,)), ((), ())), preferred_element_type=F32
            )
            for half in range(2):
                cut = term[:, half * BLK : (half + 1) * BLK].reshape((4, 2, 4, 8, BLK))
                for which in range(2):
                    terms[n, which, part, :, half * 4 : half * 4 + 4] = cut[:, which]

    def compute(step):
        def one(n, carry):
            bank(n, step)
            return carry

        lax.fori_loop(2 * step, 2 * step + 2, one, 0)
        if step == 0:
            pl.semaphore_wait(barrier, len(partners))
        for n in (2 * step, 2 * step + 1):
            pair_copy(n).start()

    def first_copies(step, axis, parts, first, send, recv):
        return [
            remote(
                parts.at[step, at(axis, by)], first.at[step, n], send.at[step, n], recv.at[step, n], near[axis, by]
            )
            for n, by in enumerate((2, 1, 3))
        ]

    @functools.cache
    def group_a(step):
        return first_copies(step, "x", parts_a, first_a, s_a1, r_a1)

    @functools.cache
    def group_b(step):
        return first_copies(step, "y", parts_b, first_b, s_b1, r_b1)

    @functools.cache
    def c1_copy(step):
        return along_z(step, parts_c, first_c, s_c1, r_c1)

    def pair_sum(step):
        for h in range(2):
            n = 2 * step + h
            pair_copy(n).wait_recv()
            for part in range(2):
                both = terms[n, core, part] + pair[n, part]
                row = 2 * h + part
                parts_a[step, :, row] = both[:, A]
                parts_b[step, row] = both[:, B]
                parts_c[step, :, row] = both[:, C]
        go(group_a(step) + group_b(step))
        if step != 3:
            go([c1_copy(step)])

    def spread(source, axis, slots, send, recv):
        return [
            remote(source.at[at(axis, by)], slots.at[n], send.at[n], recv.at[n], near[axis, by])
            for n, by in enumerate((2, 1, 3))
        ]

    def along_z(step, source, slots, send, recv):
        return remote(source.at[step], slots.at[step], send.at[step], recv.at[step], near["z", STEPS[step]])

    @functools.cache
    def a2_copy(step):
        return along_z(step, own1_a, second_a, s_a2, r_a2)

    @functools.cache
    def a3_copies():
        return spread(own2_a, "y", last_a, s_a3, r_a3)

    @functools.cache
    def b2_copy(step):
        return along_z(step, own1_b, second_b, s_b2, r_b2)

    @functools.cache
    def b3_copies():
        return spread(own2_b, "x", last_b, s_b3, r_b3)

    @functools.cache
    def c2_copies():
        return spread(own1_c, "x", second_c, s_c2, r_c2)

    @functools.cache
    def c3_copies():
        return spread(own2_c, "y", last_c, s_c3, r_c3)

    def arrived(copies):
        for copy in copies:
            copy.wait_recv()

    def finish_first(step):
        arrived(group_a(step))
        total = parts_a[step, x]
        for n in range(3):
            total = total + first_a[step, n]
        own1_a[step] = total
        if step != 3:
            go([a2_copy(step)])
        arrived(group_b(step))
        total = parts_b[step, y]
        for n in range(3):
            total = total + first_b[step, n]
        own1_b[step] = total
        if step != 3:
            go([b2_copy(step)])

    compute(0)
    compute(1)
    pair_sum(0)
    compute(2)
    pair_sum(1)
    compute(3)
    pair_sum(2)
    pair_sum(3)
    finish_first(0)
    finish_first(1)
    arrived([c1_copy(step) for step in range(3)])
    own1_c[...] = parts_c[3] + first_c[0] + first_c[1] + first_c[2]
    go(c2_copies())
    finish_first(2)
    finish_first(3)
    arrived([a2_copy(step) for step in range(3)])
    own2_a[...] = own1_a[3] + second_a[0] + second_a[1] + second_a[2]
    go(a3_copies())
    arrived([b2_copy(step) for step in range(3)])
    own2_b[...] = own1_b[3] + second_b[0] + second_b[1] + second_b[2]
    go(b3_copies())
    arrived(c2_copies())
    own2_c[...] = own1_c[x] + second_c[0] + second_c[1] + second_c[2]
    go(c3_copies())
    arrived(a3_copies())
    share[tm, A] = own2_a[y] + last_a[0] + last_a[1] + last_a[2]
    arrived(b3_copies())
    share[tm, B] = own2_b[x] + last_b[0] + last_b[1] + last_b[2]
    arrived(c3_copies())
    share[tm, C] = own2_c[y] + last_c[0] + last_c[1] + last_c[2]

    gathers = [
        remote(share.at[tm], share.at[tm], s_all.at[n], r_all.at[n], to) for n, to in enumerate((twin, side, cross))
    ]
    for copy in gathers:
        copy.start()
    for n in range(BANKS):
        pair_copy(n).wait_send()
    for copy in started:
        copy.wait_send()
    for copy in gathers:
        copy.wait_recv()
    for t in range(TMS):
        for half in range(2):
            for r in range(4):
                rows = slice(t * 32 + r * 8, t * 32 + r * 8 + 8)
                out_ref[rows, half * BLK : (half + 1) * BLK] = share[t, half * 4 + r]
    for copy in gathers:
        copy.wait_send()


def beam_banks(left, right, sums):
    tile = (8, BLK)
    vmem = lambda *dims: pltpu.VMEM(dims + tile, F32)
    dma = lambda *dims: pltpu.SemaphoreType.DMA(dims)
    scratch = [
        pltpu.VMEM((NWEIGHT, BEAMS, 2 * BLK), BF16),
        pltpu.VMEM((BEAMS, NWEIGHT * BLK), BF16),
        pltpu.VMEM((2, BEAMS, NWEIGHT * BLK), BF16),
        vmem(BANKS, 2, 2, 4, 8),
        vmem(BANKS, 2, 4, 8),
    ]
    scratch += [vmem(4, 4, 4, 3), vmem(4, 3, 4, 3), vmem(4, 4, 3), vmem(3, 4, 3), vmem(4, 3), vmem(3, 3)]
    scratch += [vmem(4, 4, 4, 3), vmem(4, 3, 4, 3), vmem(4, 4, 3), vmem(3, 4, 3), vmem(4, 3), vmem(3, 3)]
    scratch += [vmem(4, 4, 4, 2), vmem(3, 4, 4, 2), vmem(4, 4, 2), vmem(3, 4, 2), vmem(4, 2), vmem(3, 2)]
    scratch += [vmem(TMS, 8)]
    sems = [dma(BANKS), dma(4, 3), dma(3), dma(3), dma(4, 3), dma(3), dma(3), dma(3), dma(3), dma(3), dma(3)]
    return pl.pallas_call(
        beams_kernel,
        in_specs=[pl.BlockSpec(memory_space=pltpu.VMEM)] * 3,
        out_specs=pl.BlockSpec(memory_space=pltpu.VMEM),
        out_shape=jax.ShapeDtypeStruct((BLK, BEAMS), F32),
        scratch_shapes=scratch + sems + sems,
        compiler_params=pltpu.CompilerParams(
            collective_id=1, has_side_effects=True, vmem_limit_bytes=24 * MIB
        ),
        name="beams",
    )(left, right, sums)


def local(visibilities, model, beam_left, beam_right, weight_index, target_bank, widths):
    vis = visibilities.reshape((MATS, 2, N, N))
    mod = model.reshape((MATS, 2, N, N))
    inverse, vis = inverse_gains(widths, vis, mod)
    sums = calibrated_sums(weight_index, target_bank.reshape((MATS, 16)), inverse, vis)
    return beam_banks(beam_left, beam_right, sums)


def solution(mesh):
    return jax.shard_map(
        local,
        mesh=mesh,
        in_specs=(
            P("chan", "tm", None, None, None),
            P("chan", "tm", None, None, None),
            P(),
            P(),
            P("chan", None),
            P("chan", "tm", None),
            P("chan"),
        ),
        out_specs=P("chan", None),
        check_vma=False,
    )
```

time: 62.4 us -> 53.5 us (0.86)
  Pallas kernels: 61.5 us -> 52.6 us
    pallas_call x1, Pallas kernels: 34.3 us -> 27.5 us  [beam_banks(): pl.pallas_call(beams_kernel, in_specs=[pl.BlockSpec(memory_space=pltpu.VM...]
    pallas_call x1, Pallas kernels: 7.14 us -> 5.17 us  [calibrated_sums(): pl.pallas_call(sums_kernel, in_specs=[hbm, hbm, vmem, vmem], out_specs=vm...]
where the time goes in v3:
time: 53.5 us; the launch traced here: 53.3 us
  Pallas kernels  52.6 us (98%)
  local copies, waits for them, and re-layouts  0.67 us (1%)
    pallas_call x1, Pallas kernels, beam_banks(): pl.pallas_call(beams_kernel, in_specs=[pl.BlockSpec(memory_space=pltpu.VM...  27.5 us
    pallas_call x1, Pallas kernels, inverse_gains(): pl.pallas_call(gains_kernel, in_specs=[hbm, hbm, hbm], out_specs=[vmem, v...  19.9 us
    pallas_call x1, Pallas kernels, calibrated_sums(): pl.pallas_call(sums_kernel, in_specs=[hbm, hbm, vmem, vmem], out_specs=vm...  5.17 us

profile of v3, /device:TPU:1, one launch (start us, length us, event | category | flops | bytes accessed | tf_op | source)
XLA Modules:
  0.0 53.3 jit_solution(8785942917562649136)
XLA Ops:
  0.0 19.9 %gains.1 = (f32[2,8,512]{2,1,0:T(8,128)S(1)}, bf16[8,2,512,512]{3,2,1,0:T(8,128)(2,1)S(1)}) custom-call(s32[2]{0:T(128)} %width_hbm.1, bf16[8,2,512,512]{3,2,1,0:T(8,128)(2,1)} %bitcast.3, bf16[8,2,512,512]{3,2,1,0:T(8,128)(2,1)} %bitcast.4), custom_call_target="tpu_custom_call" | custom-call | tf_op jit(solution)/shard_map/gains/pallas_call | solution.py:210
  19.9 0.0 copy-start
  19.9 0.0 copy-start.1
  19.9 5.2 %sums.1.sums_ref = f32[64,128,256]{2,1,0:T(8,128)S(1)} custom-call(s32[2,16]{1,0:T(2,128)} %weight_hbm.1, s32[8,16]{1,0:T(8,128)} %bitcast.5, f32[2,8,512]{2,1,0:T(8,128)S(1)} %get-tuple-element.7.inv_ref, bf16[8,2,512,512]{3,2,1,0:T(8,128)(2,1)S(1)} %get-tuple-element.8.vis_ref), custom_call_target="tpu_custom_call" | custom-call | tf_op jit(solution)/shard_map/sums/pallas_call | solution.py:307
  25.1 0.0 copy-done
  25.1 0.0 copy-done.1
  25.1 27.5 %beams.1 = f32[128,256]{1,0:T(8,128)S(1)} custom-call(bf16[8,256,128]{2,1,0:T(8,128)(2,1)S(1)} %copy-done, bf16[8,256,128]{2,1,0:T(8,128)(2,1)S(1)} %copy-done.1, f32[64,128,256]{2,1,0:T(8,128)S(1)} %sums.1.sums_ref), custom_call_target="tpu_custom_call" | custom-call | tf_op jit(solution)/shard_map/beams/pallas_call | solution.py:570
  52.7 0.7 %copy.9 = f32[128,256]{1,0:T(8,128)} copy(f32[128,256]{1,0:T(8,128)S(1)} %beams.1) | data formatting | bytes 262144
Async XLA Ops:
  19.9 5.2 %copy-start = (bf16[8,256,128]{2,1,0:T(8,128)(2,1)S(1)}, bf16[8,256,128]{2,1,0:T(8,128)(2,1)}, u32[]{:S(2)}) copy-start(bf16[8,256,128]{2,1,0:T(8,128)(2,1)} %left_ref.1) | copy-start | bytes 1572868
  19.9 5.2 %copy-start.1 = (bf16[8,256,128]{2,1,0:T(8,128)(2,1)S(1)}, bf16[8,256,128]{2,1,0:T(8,128)(2,1)}, u32[]{:S(2)}) copy-start(bf16[8,256,128]{2,1,0:T(8,128)(2,1)} %right_ref.1) | copy-start | bytes 1572868

commit v4 on v3

--- a/solution.py
+++ b/solution.py
@@ -34,7 +34,7 @@
 
 def gains_kernel(
     width_hbm, vis_hbm, mod_hbm, inv_ref, vis_ref,
-    mod, cross_0, cross_1, power_0, power_1, sums_1, mine, halo, width, load_sem, width_sem, send_sem, recv_sem,
+    mod, cross_0, cross_1, power_0, power_1, mine, halo, width, load_sem, width_sem, send_sem, recv_sem,
 ):
     me = lax.axis_index("tm")
     chan = lax.axis_index("chan")
@@ -56,9 +56,9 @@
     width_copy = pltpu.make_async_copy(width_hbm, width, width_sem)
     width_copy.start()
 
-    row = lax.broadcasted_iota(jnp.int32, (MATS, N), 0)
-    zeros = jnp.zeros((MATS, N), F32)
-    strip = 32
+    row = lax.broadcasted_iota(jnp.int32, (LT, N), 0)
+    zeros = jnp.zeros((LT, N), F32)
+    strip = 16
     strips = N // strip
 
     def form(m, slot, top, cross, power):
@@ -75,37 +75,45 @@
         power[slot, rows, :] = size
         return [jnp.sum(one.reshape((strip // 8, 8, N)), axis=0) for one in (cross_re, cross_im, size)]
 
-    def spread(totals, sums, m):
-        here = row == m
+    def spread(totals, sums, slot):
+        here = row == slot
         return tuple(
             jnp.where(here, jnp.sum(total, axis=0, keepdims=True), old) for total, old in zip(totals, sums)
         )
 
-    def form_whole(m, sums):
+    def loaded(m):
         for copy in load(m):
             copy.wait()
+
+    def form_whole(m, sums):
+        loaded(m)
         totals = [jnp.zeros((8, N), F32) for _ in range(3)]
         for top in range(0, N, strip):
             totals = [old + new for old, new in zip(totals, form(m, m, top, cross_0, power_0))]
         return spread(totals, sums, m)
 
-    def sweep(k, gains, first, cross, power):
+    def sweep(k, gains, cross, power, beside=lambda piece: None):
         gain_re, gain_im = gains
         size = gain_re * gain_re + gain_im * gain_im
-        by_row = jnp.transpose(size)
+        by_row = jnp.transpose(jnp.concatenate([size, size], axis=0))
         both = jnp.concatenate([*split(gain_re), *split(gain_im)], axis=0).astype(BF16)
         num_re, num_im, den = zeros, zeros, zeros
         for m in range(LT):
-            with_re = jnp.dot(both, cross[m, 0], preferred_element_type=F32)
-            with_im = jnp.dot(both, cross[m, 1], preferred_element_type=F32)
-            one_re = (with_re[0:8] + with_re[8:16]) - (with_im[16:24] + with_im[24:32])
-            one_im = (with_im[0:8] + with_im[8:16]) + (with_re[16:24] + with_re[24:32])
+            halves = []
+            for part in range(2):
+                for half in range(2):
+                    columns = cross[m, part, :, half * (N // 2) : (half + 1) * (N // 2)]
+                    halves.append(jnp.dot(both, columns, preferred_element_type=F32))
+                    beside(4 * m + 2 * part + half)
+            with_re = jnp.concatenate(halves[0:2], axis=1)
+            with_im = jnp.concatenate(halves[2:4], axis=1)
+            one_re = (with_re[0:4] + with_re[4:8]) - (with_im[8:12] + with_im[12:16])
+            one_im = (with_im[0:4] + with_im[4:8]) + (with_re[8:12] + with_re[12:16])
             total = jnp.zeros((8, N), F32)
             for top in range(0, N, strip):
                 rows = slice(top, top + strip)
-                by = by_row[rows, first + m : first + m + 1]
-                total = total + jnp.sum((by * power[m, rows, :]).reshape((strip // 8, 8, N)), axis=0)
-            here = row == first + m
+                total = total + jnp.sum((by_row[rows, m : m + 1] * power[m, rows, :]).reshape((strip // 8, 8, N)), axis=0)
+            here = row == m
             num_re = jnp.where(here, one_re, num_re)
             num_im = jnp.where(here, one_im, num_im)
             den = jnp.where(here, jnp.sum(total, axis=0, keepdims=True), den)
@@ -113,42 +121,37 @@
         new_re = num_re / den
         new_im = num_im / den
         odd = lax.rem(k, 2) == 1
-        new_re = jnp.where(odd, 0.5 * (new_re + gain_re), new_re)
-        new_im = jnp.where(odd, 0.5 * (new_im + gain_im), new_im)
-        mine = (row >= first) & (row < first + LT)
-        return jnp.where(mine, new_re, gain_re), jnp.where(mine, new_im, gain_im)
+        return jnp.where(odd, 0.5 * (new_re + gain_re), new_re), jnp.where(odd, 0.5 * (new_im + gain_im), new_im)
 
     num_re, num_im, den = lax.fori_loop(0, LT, form_whole, (zeros, zeros, zeros))
     den = den + epsilon
-    sums_1[...] = jnp.zeros_like(sums_1)
-    units = -(-LT * strips // (ITERS - 1))
-
-    def beside(k, gains):
-        @pl.when(k <= LT)
-        def _():
-            for copy in load(LT + k - 1):
-                copy.wait()
-
-        new = sweep(k, gains, 0, cross_0, power_0)
-        for i in range(units):
-            unit = (k - 1) * units + i
-            real = unit < LT * strips
-            unit = jnp.minimum(unit, LT * strips - 1)
-            slot = lax.div(unit, strips)
-            top = pl.multiple_of(lax.rem(unit, strips) * strip, strip)
-            for n, total in enumerate(form(LT + slot, slot, top, cross_1, power_1)):
-                sums_1[slot, n] += jnp.where(real, total, 0.0)
-        return new
-
-    gains = lax.fori_loop(1, ITERS, beside, (num_re / den, num_im / den))
+    gains_0 = (num_re / den, num_im / den)
     sums = (zeros, zeros, zeros)
-    for m in range(LT):
-        sums = spread([sums_1[m, n] for n in range(3)], sums, LT + m)
+    totals = []
+    pieces = (ITERS - 1) * LT * 4
+
+    for k in range(1, ITERS):
+        if k <= LT:
+            loaded(LT + k - 1)
+
+        def more(piece):
+            nonlocal sums, totals
+            piece += (k - 1) * LT * 4
+            for unit in range(piece * LT * strips // pieces, (piece + 1) * LT * strips // pieces):
+                slot, part = divmod(unit, strips)
+                new = form(LT + slot, slot, part * strip, cross_1, power_1)
+                totals = new if part == 0 else [old + one for old, one in zip(totals, new)]
+                if part == strips - 1:
+                    sums = spread(totals, sums, slot)
+
+        gains_0 = sweep(k, gains_0, cross_0, power_0, more)
+
     num_re, num_im, den = sums
     den = den + epsilon
-    later = row >= LT
-    gains = (jnp.where(later, num_re / den, gains[0]), jnp.where(later, num_im / den, gains[1]))
-    gain_re, gain_im = lax.fori_loop(1, ITERS, lambda k, gains: sweep(k, gains, LT, cross_1, power_1), gains)
+    gains_1 = lax.fori_loop(
+        1, ITERS, lambda k, gains: sweep(k, gains, cross_1, power_1), (num_re / den, num_im / den)
+    )
+    gain_re, gain_im = (jnp.concatenate(pair, axis=0) for pair in zip(gains_0, gains_1))
     first_re = gain_re[:, 0:1]
     first_im = gain_im[:, 0:1]
     divisor = jnp.maximum(jnp.sqrt(first_re * first_re + first_im * first_im), 1.0)
@@ -172,6 +175,7 @@
     for copy in copies:
         copy.start()
     width_copy.wait()
+    row = lax.broadcasted_iota(jnp.int32, (MATS, N), 0)
     within = lax.rem(row, LT)
     interval = me * LT + within
     half_width = jnp.where(row < LT, width[0], width[1])
@@ -221,7 +225,6 @@
             pltpu.VMEM((LT, 2, N, N), BF16),
             pltpu.VMEM((LT, N, N), F32),
             pltpu.VMEM((LT, N, N), F32),
-            pltpu.VMEM((LT, 3, 8, N), F32),
             pltpu.VMEM((2, MATS, N), F32),
             pltpu.VMEM((2, 2, MATS, N), F32),
             pltpu.SMEM((LC,), jnp.int32),
@@ -271,6 +274,7 @@
             for i in range(groups):
                 place = bank[m, i * groups + j] * NWEIGHT + weight[c, i * groups + j]
                 scale = jnp.dot(by_row[i * BLK : (i + 1) * BLK, :], by_col[j], preferred_element_type=F32)
+                ones = []
                 for s in range(0, BLK, strip):
                     rows = slice(i * BLK + s, i * BLK + s + strip)
                     to = slice(s, s + strip)
@@ -278,8 +282,10 @@
                     vis_im = vis_ref[m, 1, rows, cols].astype(F32)
                     one_re = scale[to, 0:BLK]
                     one_im = scale[to, BLK : 2 * BLK]
-                    out_ref[place, to, 0:BLK] += one_re * vis_re - one_im * vis_im
-                    out_ref[place, to, BLK : 2 * BLK] += one_re * vis_im + one_im * vis_re
+                    ones.append((to, one_re * vis_re - one_im * vis_im, one_re * vis_im + one_im * vis_re))
+                for to, one_re, one_im in ones:
+                    out_ref[place, to, 0:BLK] += one_re
+                    out_ref[place, to, BLK : 2 * BLK] += one_im
 
     def clear(k, carry):
         out_ref[k] = jnp.zeros((BLK, 2 * BLK), F32)
@@ -357,12 +363,14 @@
 
     near = {(axis, by): device({**place, axis: at(axis, by)}) for axis in "xyz" for by in (1, 2, 3)}
     twin = device(place, 1 - core)
-    other_low = lax.div(x, 2) * 2 + (1 - x_low)
-    side = device({**place, "x": other_low})
-    cross = device({**place, "x": other_low}, 1 - core)
+    x_pair = lax.div(x, 2) * 2
+    x_other = 2 - x_pair
+    side = {**place, "x": x_pair + 1 - x_low}
+    beside = [device({**side, "y": at("y", by)}) for by in range(4)]
+    others = [device({**place, "x": x_other + x_low}), device({**place, "x": x_other + 1 - x_low})]
 
     barrier = pltpu.get_barrier_semaphore()
-    partners = [twin, cross, *near.values()]
+    partners = [twin, *beside[1:], *near.values()]
     for other in partners:
         pl.semaphore_signal(barrier, inc=1, device_id=other, device_id_type=MESH)
 
@@ -403,15 +411,17 @@
                     terms[n, which, part, :, half * 4 : half * 4 + 4] = cut[:, which]
 
     def compute(step):
+        if step == 0:
+            bank(0, 0)
+            pl.semaphore_wait(barrier, len(partners))
+            pair_copy(0).start()
+
         def one(n, carry):
             bank(n, step)
+            pair_copy(n).start()
             return carry
 
-        lax.fori_loop(2 * step, 2 * step + 2, one, 0)
-        if step == 0:
-            pl.semaphore_wait(barrier, len(partners))
-        for n in (2 * step, 2 * step + 1):
-            pair_copy(n).start()
+        lax.fori_loop(max(2 * step, 1), 2 * step + 2, one, 0)
 
     def first_copies(step, axis, parts, first, send, recv):
         return [
@@ -460,9 +470,14 @@
     def a2_copy(step):
         return along_z(step, own1_a, second_a, s_a2, r_a2)
 
+    def both_chips(source, slots, send, recv):
+        copy = lambda n, by, slot, to: remote(source.at[at("y", by)], slots.at[slot], send.at[n], recv.at[n], to)
+        made = [copy(n, by, n, near["y", by]) for n, by in enumerate((2, 1, 3))]
+        return made + [copy(3 + by, by, 3 + by, beside[by]) for by in (2, 1, 3, 0)]
+
     @functools.cache
     def a3_copies():
-        return spread(own2_a, "y", last_a, s_a3, r_a3)
+        return both_chips(own2_a, last_a, s_a3, r_a3)
 
     @functools.cache
     def b2_copy(step):
@@ -470,7 +485,11 @@
 
     @functools.cache
     def b3_copies():
-        return spread(own2_b, "x", last_b, s_b3, r_b3)
+        pairs = ((x_other, others[1]), (x_other, others[0]), (x_pair, beside[0]))
+        return [
+            remote(own2_b.at[pl.ds(at_x, 2)], last_b.at[n], s_b3.at[n], r_b3.at[n], to)
+            for n, (at_x, to) in enumerate(pairs)
+        ]
 
     @functools.cache
     def c2_copies():
@@ -478,7 +497,7 @@
 
     @functools.cache
     def c3_copies():
-        return spread(own2_c, "y", last_c, s_c3, r_c3)
+        return both_chips(own2_c, last_c, s_c3, r_c3)
 
     def arrived(copies):
         for copy in copies:
@@ -510,10 +529,10 @@
     pair_sum(3)
     finish_first(0)
     finish_first(1)
+    finish_first(2)
     arrived([c1_copy(step) for step in range(3)])
     own1_c[...] = parts_c[3] + first_c[0] + first_c[1] + first_c[2]
     go(c2_copies())
-    finish_first(2)
     finish_first(3)
     arrived([a2_copy(step) for step in range(3)])
     own2_a[...] = own1_a[3] + second_a[0] + second_a[1] + second_a[2]
@@ -524,16 +543,19 @@
     arrived(c2_copies())
     own2_c[...] = own1_c[x] + second_c[0] + second_c[1] + second_c[2]
     go(c3_copies())
+
+    def settle(tiles, source, slots):
+        share[core, x_low, tiles] = source[y] + slots[0] + slots[1] + slots[2]
+        share[core, 1 - x_low, tiles] = slots[3] + slots[4] + slots[5] + slots[6]
+
     arrived(a3_copies())
-    share[tm, A] = own2_a[y] + last_a[0] + last_a[1] + last_a[2]
+    settle(A, own2_a, last_a)
     arrived(b3_copies())
-    share[tm, B] = own2_b[x] + last_b[0] + last_b[1] + last_b[2]
+    share[core, :, B] = own2_b[pl.ds(x_pair, 2)] + last_b[0] + last_b[1] + last_b[2]
     arrived(c3_copies())
-    share[tm, C] = own2_c[y] + last_c[0] + last_c[1] + last_c[2]
-
-    gathers = [
-        remote(share.at[tm], share.at[tm], s_all.at[n], r_all.at[n], to) for n, to in enumerate((twin, side, cross))
-    ]
+    settle(C, own2_c, last_c)
+
+    gathers = [remote(share.at[core], share.at[core], s_all, r_all, twin)]
     for copy in gathers:
         copy.start()
     for n in range(BANKS):
@@ -546,7 +568,7 @@
         for half in range(2):
             for r in range(4):
                 rows = slice(t * 32 + r * 8, t * 32 + r * 8 + 8)
-                out_ref[rows, half * BLK : (half + 1) * BLK] = share[t, half * 4 + r]
+                out_ref[rows, half * BLK : (half + 1) * BLK] = share[t % 2, t // 2, half * 4 + r]
     for copy in gathers:
         copy.wait_send()
 
@@ -562,11 +584,12 @@
         vmem(BANKS, 2, 2, 4, 8),
         vmem(BANKS, 2, 4, 8),
     ]
-    scratch += [vmem(4, 4, 4, 3), vmem(4, 3, 4, 3), vmem(4, 4, 3), vmem(3, 4, 3), vmem(4, 3), vmem(3, 3)]
-    scratch += [vmem(4, 4, 4, 3), vmem(4, 3, 4, 3), vmem(4, 4, 3), vmem(3, 4, 3), vmem(4, 3), vmem(3, 3)]
-    scratch += [vmem(4, 4, 4, 2), vmem(3, 4, 4, 2), vmem(4, 4, 2), vmem(3, 4, 2), vmem(4, 2), vmem(3, 2)]
-    scratch += [vmem(TMS, 8)]
-    sems = [dma(BANKS), dma(4, 3), dma(3), dma(3), dma(4, 3), dma(3), dma(3), dma(3), dma(3), dma(3), dma(3)]
+    scratch += [vmem(4, 4, 4, 3), vmem(4, 3, 4, 3), vmem(4, 4, 3), vmem(3, 4, 3), vmem(4, 3), vmem(7, 3)]
+    scratch += [vmem(4, 4, 4, 3), vmem(4, 3, 4, 3), vmem(4, 4, 3), vmem(3, 4, 3), vmem(4, 3), vmem(3, 2, 3)]
+    scratch += [vmem(4, 4, 4, 2), vmem(3, 4, 4, 2), vmem(4, 4, 2), vmem(3, 4, 2), vmem(4, 2), vmem(7, 2)]
+    scratch += [vmem(2, 2, 8)]
+    sems = [dma(BANKS), dma(4, 3), dma(3), dma(7), dma(4, 3), dma(3), dma(3), dma(3), dma(3), dma(7)]
+    sems += [pltpu.SemaphoreType.DMA]
     return pl.pallas_call(
         beams_kernel,
         in_specs=[pl.BlockSpec(memory_space=pltpu.VMEM)] * 3,

time: 53.5 us -> 52 us (0.972)
  Pallas kernels: 52.6 us -> 51.2 us
    pallas_call x1, Pallas kernels: 19.9 us -> 18.5 us  [inverse_gains(): pl.pallas_call(gains_kernel, in_specs=[hbm, hbm, hbm], out_specs=[vmem, v...]
where the time goes in v4:
time: 52 us; the launch traced here: 51.9 us
  Pallas kernels  51.2 us (98%)
  local copies, waits for them, and re-layouts  0.67 us (1%)
    pallas_call x1, Pallas kernels, beam_banks(): pl.pallas_call(beams_kernel, in_specs=[pl.BlockSpec(memory_space=pltpu.VM...  27.5 us
    pallas_call x1, Pallas kernels, inverse_gains(): pl.pallas_call(gains_kernel, in_specs=[hbm, hbm, hbm], out_specs=[vmem, v...  18.5 us
    pallas_call x1, Pallas kernels, calibrated_sums(): pl.pallas_call(sums_kernel, in_specs=[hbm, hbm, vmem, vmem], out_specs=vm...  5.15 us

profile of v4, /device:TPU:1, one launch (start us, length us, event | category | flops | bytes accessed | tf_op | source)
XLA Modules:
  0.0 51.9 jit_solution(7874572509530435700)
XLA Ops:
  0.0 18.5 %gains.1 = (f32[2,8,512]{2,1,0:T(8,128)S(1)}, bf16[8,2,512,512]{3,2,1,0:T(8,128)(2,1)S(1)}) custom-call(s32[2]{0:T(128)} %width_hbm.1, bf16[8,2,512,512]{3,2,1,0:T(8,128)(2,1)} %bitcast.3, bf16[8,2,512,512]{3,2,1,0:T(8,128)(2,1)} %bitcast.4), custom_call_target="tpu_custom_call" | custom-call | tf_op jit(solution)/shard_map/gains/pallas_call | solution.py:214
  18.5 0.0 copy-start
  18.6 0.0 copy-start.1
  18.6 5.2 %sums.1.sums_ref = f32[64,128,256]{2,1,0:T(8,128)S(1)} custom-call(s32[2,16]{1,0:T(2,128)} %weight_hbm.1, s32[8,16]{1,0:T(8,128)} %bitcast.5, f32[2,8,512]{2,1,0:T(8,128)S(1)} %get-tuple-element.7.inv_ref, bf16[8,2,512,512]{3,2,1,0:T(8,128)(2,1)S(1)} %get-tuple-element.8.vis_ref), custom_call_target="tpu_custom_call" | custom-call | tf_op jit(solution)/shard_map/sums/pallas_call | solution.py:313
  23.7 0.0 copy-done
  23.7 0.0 copy-done.1
  23.8 27.5 %beams.1 = f32[128,256]{1,0:T(8,128)S(1)} custom-call(bf16[8,256,128]{2,1,0:T(8,128)(2,1)S(1)} %copy-done, bf16[8,256,128]{2,1,0:T(8,128)(2,1)S(1)} %copy-done.1, f32[64,128,256]{2,1,0:T(8,128)S(1)} %sums.1.sums_ref), custom_call_target="tpu_custom_call" | custom-call | tf_op jit(solution)/shard_map/beams/pallas_call | solution.py:593
  51.3 0.7 %copy.9 = f32[128,256]{1,0:T(8,128)} copy(f32[128,256]{1,0:T(8,128)S(1)} %beams.1) | data formatting | bytes 262144
Async XLA Ops:
  18.5 5.2 %copy-start = (bf16[8,256,128]{2,1,0:T(8,128)(2,1)S(1)}, bf16[8,256,128]{2,1,0:T(8,128)(2,1)}, u32[]{:S(2)}) copy-start(bf16[8,256,128]{2,1,0:T(8,128)(2,1)} %left_ref.1) | copy-start | bytes 1572868
  18.6 5.2 %copy-start.1 = (bf16[8,256,128]{2,1,0:T(8,128)(2,1)S(1)}, bf16[8,256,128]{2,1,0:T(8,128)(2,1)}, u32[]{:S(2)}) copy-start(bf16[8,256,128]{2,1,0:T(8,128)(2,1)} %right_ref.1) | copy-start | bytes 1572868

commit v5 on v4

--- a/solution.py
+++ b/solution.py
@@ -19,6 +19,8 @@
 TMS = 4
 ALL_T = 16
 MATS = LC * LT
+EXACT = 4
+FINE = 256
 MESH = pl.DeviceIdType.MESH
 MIB = 1024 * 1024
 F32 = jnp.float32
@@ -34,7 +36,7 @@
 
 def gains_kernel(
     width_hbm, vis_hbm, mod_hbm, inv_ref, vis_ref,
-    mod, cross_0, cross_1, power_0, power_1, mine, halo, width, load_sem, width_sem, send_sem, recv_sem,
+    mod, cross_0, cross_1, low_0, low_1, power_0, power_1, mine, halo, width, load_sem, width_sem, send_sem, recv_sem,
 ):
     me = lax.axis_index("tm")
     chan = lax.axis_index("chan")
@@ -61,8 +63,9 @@
     strip = 16
     strips = N // strip
 
-    def form(m, slot, top, cross, power):
+    def form(m, slot, top, cross, low, power):
         rows = pl.ds(top, strip)
+        fine = top < FINE
         vis_re = vis_ref[m, 0, rows, :].astype(F32)
         vis_im = vis_ref[m, 1, rows, :].astype(F32)
         mod_re = mod[m, 0, rows, :].astype(F32)
@@ -70,8 +73,11 @@
         cross_re = mod_re * vis_re + mod_im * vis_im
         cross_im = mod_im * vis_re - mod_re * vis_im
         size = mod_re * mod_re + mod_im * mod_im
-        cross[slot, 0, rows, :] = cross_re.astype(BF16)
-        cross[slot, 1, rows, :] = cross_im.astype(BF16)
+        for part, one in enumerate((cross_re, cross_im)):
+            rounded = one.astype(BF16)
+            cross[slot, part, rows, :] = rounded
+            if fine:
+                low[slot, part, rows, :] = (one - rounded.astype(F32)).astype(BF16)
         power[slot, rows, :] = size
         return [jnp.sum(one.reshape((strip // 8, 8, N)), axis=0) for one in (cross_re, cross_im, size)]
 
@@ -89,10 +95,10 @@
         loaded(m)
         totals = [jnp.zeros((8, N), F32) for _ in range(3)]
         for top in range(0, N, strip):
-            totals = [old + new for old, new in zip(totals, form(m, m, top, cross_0, power_0))]
+            totals = [old + new for old, new in zip(totals, form(m, m, top, cross_0, low_0, power_0))]
         return spread(totals, sums, m)
 
-    def sweep(k, gains, cross, power, beside=lambda piece: None):
+    def sweep(k, gains, cross, low, power, exact, beside=lambda piece: None):
         gain_re, gain_im = gains
         size = gain_re * gain_re + gain_im * gain_im
         by_row = jnp.transpose(jnp.concatenate([size, size], axis=0))
@@ -102,8 +108,11 @@
             halves = []
             for part in range(2):
                 for half in range(2):
-                    columns = cross[m, part, :, half * (N // 2) : (half + 1) * (N // 2)]
-                    halves.append(jnp.dot(both, columns, preferred_element_type=F32))
+                    columns = slice(half * (N // 2), (half + 1) * (N // 2))
+                    one = jnp.dot(both, cross[m, part, :, columns], preferred_element_type=F32)
+                    if exact:
+                        one = one + jnp.dot(both[:, 0:FINE], low[m, part, :, columns], preferred_element_type=F32)
+                    halves.append(one)
                     beside(4 * m + 2 * part + half)
             with_re = jnp.concatenate(halves[0:2], axis=1)
             with_im = jnp.concatenate(halves[2:4], axis=1)
@@ -139,18 +148,20 @@
             piece += (k - 1) * LT * 4
             for unit in range(piece * LT * strips // pieces, (piece + 1) * LT * strips // pieces):
                 slot, part = divmod(unit, strips)
-                new = form(LT + slot, slot, part * strip, cross_1, power_1)
+                new = form(LT + slot, slot, part * strip, cross_1, low_1, power_1)
                 totals = new if part == 0 else [old + one for old, one in zip(totals, new)]
                 if part == strips - 1:
                     sums = spread(totals, sums, slot)
 
-        gains_0 = sweep(k, gains_0, cross_0, power_0, more)
+        gains_0 = sweep(k, gains_0, cross_0, low_0, power_0, k == EXACT, more)
 
     num_re, num_im, den = sums
     den = den + epsilon
-    gains_1 = lax.fori_loop(
-        1, ITERS, lambda k, gains: sweep(k, gains, cross_1, power_1), (num_re / den, num_im / den)
-    )
+    gains_1 = (num_re / den, num_im / den)
+    rounded = lambda k, gains: sweep(k, gains, cross_1, low_1, power_1, False)
+    gains_1 = lax.fori_loop(1, EXACT, rounded, gains_1)
+    gains_1 = sweep(EXACT, gains_1, cross_1, low_1, power_1, True)
+    gains_1 = lax.fori_loop(EXACT + 1, ITERS, rounded, gains_1)
     gain_re, gain_im = (jnp.concatenate(pair, axis=0) for pair in zip(gains_0, gains_1))
     first_re = gain_re[:, 0:1]
     first_im = gain_im[:, 0:1]
@@ -223,6 +234,8 @@
             pltpu.VMEM((MATS, 2, N, N), BF16),
             pltpu.VMEM((LT, 2, N, N), BF16),
             pltpu.VMEM((LT, 2, N, N), BF16),
+            pltpu.VMEM((LT, 2, FINE, N), BF16),
+            pltpu.VMEM((LT, 2, FINE, N), BF16),
             pltpu.VMEM((LT, N, N), F32),
             pltpu.VMEM((LT, N, N), F32),
             pltpu.VMEM((2, MATS, N), F32),
@@ -234,7 +247,7 @@
             pltpu.SemaphoreType.DMA((2,)),
         ],
         compiler_params=pltpu.CompilerParams(
-            collective_id=0, has_side_effects=True, vmem_limit_bytes=34 * MIB
+            collective_id=0, has_side_effects=True, vmem_limit_bytes=36 * MIB
         ),
         name="gains",
     )(*(pltpu.with_memory_space_constraint(x, pltpu.HBM) for x in (widths, vis, mod)))
@@ -548,6 +561,11 @@
         share[core, x_low, tiles] = source[y] + slots[0] + slots[1] + slots[2]
         share[core, 1 - x_low, tiles] = slots[3] + slots[4] + slots[5] + slots[6]
 
+    for n in range(BANKS):
+        pair_copy(n).wait_send()
+    late = [*a3_copies(), *b3_copies(), *c3_copies()]
+    for copy in started[: -len(late)]:
+        copy.wait_send()
     arrived(a3_copies())
     settle(A, own2_a, last_a)
     arrived(b3_copies())
@@ -558,9 +576,7 @@
     gathers = [remote(share.at[core], share.at[core], s_all, r_all, twin)]
     for copy in gathers:
         copy.start()
-    for n in range(BANKS):
-        pair_copy(n).wait_send()
-    for copy in started:
+    for copy in late:
         copy.wait_send()
     for copy in gathers:
         copy.wait_recv()

time: 52 us -> 53.6 us (1.031)
  Pallas kernels: 51.2 us -> 52.8 us
    pallas_call x1, Pallas kernels: 18.5 us -> 20 us  [inverse_gains(): pl.pallas_call(gains_kernel, in_specs=[hbm, hbm, hbm], out_specs=[vmem, v...]
where the time goes in v5:
time: 53.6 us; the launch traced here: 53.5 us
  Pallas kernels  52.8 us (99%)
  local copies, waits for them, and re-layouts  0.67 us (1%)
    pallas_call x1, Pallas kernels, beam_banks(): pl.pallas_call(beams_kernel, in_specs=[pl.BlockSpec(memory_space=pltpu.VM...  27.6 us
    pallas_call x1, Pallas kernels, inverse_gains(): pl.pallas_call(gains_kernel, in_specs=[hbm, hbm, hbm], out_specs=[vmem, v...  20 us
    pallas_call x1, Pallas kernels, calibrated_sums(): pl.pallas_call(sums_kernel, in_specs=[hbm, hbm, vmem, vmem], out_specs=vm...  5.16 us

profile of v5, /device:TPU:1, one launch (start us, length us, event | category | flops | bytes accessed | tf_op | source)
XLA Modules:
  0.0 53.5 jit_solution(13275839428975474814)
XLA Ops:
  0.0 20.0 %gains.1 = (f32[2,8,512]{2,1,0:T(8,128)S(1)}, bf16[8,2,512,512]{3,2,1,0:T(8,128)(2,1)S(1)}) custom-call(s32[2]{0:T(128)} %width_hbm.1, bf16[8,2,512,512]{3,2,1,0:T(8,128)(2,1)} %bitcast.3, bf16[8,2,512,512]{3,2,1,0:T(8,128)(2,1)} %bitcast.4), custom_call_target="tpu_custom_call" | custom-call | tf_op jit(solution)/shard_map/gains/pallas_call | solution.py:225
  20.0 0.0 copy-start
  20.0 0.0 copy-start.1
  20.0 5.2 %sums.1.sums_ref = f32[64,128,256]{2,1,0:T(8,128)S(1)} custom-call(s32[2,16]{1,0:T(2,128)} %weight_hbm.1, s32[8,16]{1,0:T(8,128)} %bitcast.5, f32[2,8,512]{2,1,0:T(8,128)S(1)} %get-tuple-element.7.inv_ref, bf16[8,2,512,512]{3,2,1,0:T(8,128)(2,1)S(1)} %get-tuple-element.8.vis_ref), custom_call_target="tpu_custom_call" | custom-call | tf_op jit(solution)/shard_map/sums/pallas_call | solution.py:326
  25.2 0.0 copy-done
  25.2 0.0 copy-done.1
  25.2 27.6 %beams.1 = f32[128,256]{1,0:T(8,128)S(1)} custom-call(bf16[8,256,128]{2,1,0:T(8,128)(2,1)S(1)} %copy-done, bf16[8,256,128]{2,1,0:T(8,128)(2,1)S(1)} %copy-done.1, f32[64,128,256]{2,1,0:T(8,128)S(1)} %sums.1.sums_ref), custom_call_target="tpu_custom_call" | custom-call | tf_op jit(solution)/shard_map/beams/pallas_call | solution.py:609
  52.8 0.7 %copy.9 = f32[128,256]{1,0:T(8,128)} copy(f32[128,256]{1,0:T(8,128)S(1)} %beams.1) | data formatting | bytes 262144
Async XLA Ops:
  20.0 5.2 %copy-start = (bf16[8,256,128]{2,1,0:T(8,128)(2,1)S(1)}, bf16[8,256,128]{2,1,0:T(8,128)(2,1)}, u32[]{:S(2)}) copy-start(bf16[8,256,128]{2,1,0:T(8,128)(2,1)} %left_ref.1) | copy-start | bytes 1572868
  20.0 5.2 %copy-start.1 = (bf16[8,256,128]{2,1,0:T(8,128)(2,1)S(1)}, bf16[8,256,128]{2,1,0:T(8,128)(2,1)}, u32[]{:S(2)}) copy-start(bf16[8,256,128]{2,1,0:T(8,128)(2,1)} %right_ref.1) | copy-start | bytes 1572868

commit v6 on v5

--- a/solution.py
+++ b/solution.py
@@ -35,7 +35,7 @@
 
 
 def gains_kernel(
-    width_hbm, vis_hbm, mod_hbm, inv_ref, vis_ref,
+    width_hbm, vis_hbm, mod_hbm, inv_ref, vis_ref, wide_ref,
     mod, cross_0, cross_1, low_0, low_1, power_0, power_1, mine, halo, width, load_sem, width_sem, send_sem, recv_sem,
 ):
     me = lax.axis_index("tm")
@@ -63,13 +63,16 @@
     strip = 16
     strips = N // strip
 
-    def form(m, slot, top, cross, low, power):
+    def form(m, slot, top, cross, low, power, wide=None):
         rows = pl.ds(top, strip)
         fine = top < FINE
         vis_re = vis_ref[m, 0, rows, :].astype(F32)
         vis_im = vis_ref[m, 1, rows, :].astype(F32)
         mod_re = mod[m, 0, rows, :].astype(F32)
         mod_im = mod[m, 1, rows, :].astype(F32)
+        if wide is not None:
+            wide[slot, 0, rows, :] = vis_re
+            wide[slot, 1, rows, :] = vis_im
         cross_re = mod_re * vis_re + mod_im * vis_im
         cross_im = mod_im * vis_re - mod_re * vis_im
         size = mod_re * mod_re + mod_im * mod_im
@@ -95,7 +98,7 @@
         loaded(m)
         totals = [jnp.zeros((8, N), F32) for _ in range(3)]
         for top in range(0, N, strip):
-            totals = [old + new for old, new in zip(totals, form(m, m, top, cross_0, low_0, power_0))]
+            totals = [old + new for old, new in zip(totals, form(m, m, top, cross_0, low_0, power_0, wide_ref))]
         return spread(totals, sums, m)
 
     def sweep(k, gains, cross, low, power, exact, beside=lambda piece: None):
@@ -225,10 +228,11 @@
     return pl.pallas_call(
         gains_kernel,
         in_specs=[hbm, hbm, hbm],
-        out_specs=[vmem, vmem],
+        out_specs=[vmem, vmem, vmem],
         out_shape=[
             jax.ShapeDtypeStruct((2, MATS, N), F32),
             jax.ShapeDtypeStruct((MATS, 2, N, N), BF16),
+            jax.ShapeDtypeStruct((LT, 2, N, N), F32),
         ],
         scratch_shapes=[
             pltpu.VMEM((MATS, 2, N, N), BF16),
@@ -253,7 +257,7 @@
     )(*(pltpu.with_memory_space_constraint(x, pltpu.HBM) for x in (widths, vis, mod)))
 
 
-def sums_kernel(weight_hbm, bank_hbm, inv_ref, vis_ref, out_ref, weight, bank, row_a, row_b, col_a, col_b, sem):
+def sums_kernel(weight_hbm, bank_hbm, inv_ref, vis_ref, wide_ref, out_ref, weight, bank, row_a, row_b, col_a, col_b, sem):
     copies = [
         pltpu.make_async_copy(weight_hbm, weight, sem.at[0]),
         pltpu.make_async_copy(bank_hbm, bank, sem.at[1]),
@@ -281,7 +285,7 @@
             by_col[j, :, 0:BLK] = col_re[:, cols]
             by_col[j, :, BLK : 2 * BLK] = col_im[:, cols]
 
-    def add(m, c, by_row, by_col):
+    def add(m, c, by_row, by_col, vis):
         for j in range(groups):
             cols = slice(j * BLK, (j + 1) * BLK)
             for i in range(groups):
@@ -291,8 +295,8 @@
                 for s in range(0, BLK, strip):
                     rows = slice(i * BLK + s, i * BLK + s + strip)
                     to = slice(s, s + strip)
-                    vis_re = vis_ref[m, 0, rows, cols].astype(F32)
-                    vis_im = vis_ref[m, 1, rows, cols].astype(F32)
+                    vis_re = vis[m, 0, rows, cols].astype(F32)
+                    vis_im = vis[m, 1, rows, cols].astype(F32)
                     one_re = scale[to, 0:BLK]
                     one_im = scale[to, BLK : 2 * BLK]
                     ones.append((to, one_re * vis_re - one_im * vis_im, one_re * vis_im + one_im * vis_re))
@@ -309,23 +313,27 @@
     for copy in copies:
         copy.wait()
 
-    def two(q, carry):
-        c = lax.div(q, LT // 2)
+    def two(q, c, vis):
         factors(2 * q + 1, row_b, col_b)
-        add(2 * q, c, row_a, col_a)
+        add(2 * q, c, row_a, col_a, vis)
         factors(jnp.minimum(2 * q + 2, MATS - 1), row_a, col_a)
-        add(2 * q + 1, c, row_b, col_b)
-        return carry
-
-    lax.fori_loop(0, MATS // 2, two, 0)
-
-
-def calibrated_sums(weight_index, target_bank, inverse, vis):
+        add(2 * q + 1, c, row_b, col_b, vis)
+
+    for c, vis in enumerate((wide_ref, vis_ref)):
+
+        def one(q, carry):
+            two(q, c, vis)
+            return carry
+
+        lax.fori_loop(c * LT // 2, (c + 1) * LT // 2, one, 0)
+
+
+def calibrated_sums(weight_index, target_bank, inverse, vis, wide):
     hbm = pl.BlockSpec(memory_space=pltpu.HBM)
     vmem = pl.BlockSpec(memory_space=pltpu.VMEM)
     return pl.pallas_call(
         sums_kernel,
-        in_specs=[hbm, hbm, vmem, vmem],
+        in_specs=[hbm, hbm, vmem, vmem, vmem],
         out_specs=vmem,
         out_shape=jax.ShapeDtypeStruct((BANKS * NWEIGHT, BLK, 2 * BLK), F32),
         scratch_shapes=[
@@ -339,7 +347,7 @@
         ],
         compiler_params=pltpu.CompilerParams(vmem_limit_bytes=12 * MIB),
         name="sums",
-    )(*(pltpu.with_memory_space_constraint(x, pltpu.HBM) for x in (weight_index, target_bank)), inverse, vis)
+    )(*(pltpu.with_memory_space_constraint(x, pltpu.HBM) for x in (weight_index, target_bank)), inverse, vis, wide)
 
 
 STEPS = (2, 1, 3, 0)
@@ -622,8 +630,8 @@
 def local(visibilities, model, beam_left, beam_right, weight_index, target_bank, widths):
     vis = visibilities.reshape((MATS, 2, N, N))
     mod = model.reshape((MATS, 2, N, N))
-    inverse, vis = inverse_gains(widths, vis, mod)
-    sums = calibrated_sums(weight_index, target_bank.reshape((MATS, 16)), inverse, vis)
+    inverse, vis, wide = inverse_gains(widths, vis, mod)
+    sums = calibrated_sums(weight_index, target_bank.reshape((MATS, 16)), inverse, vis, wide)
     return beam_banks(beam_left, beam_right, sums)
 
 

time: 53.6 us -> 53.5 us (level)
  no operation moved by 1% of the time
where the time goes in v6:
time: 53.5 us; the launch traced here: 53.4 us
  Pallas kernels  52.7 us (99%)
  local copies, waits for them, and re-layouts  0.67 us (1%)
    pallas_call x1, Pallas kernels, beam_banks(): pl.pallas_call(beams_kernel, in_specs=[pl.BlockSpec(memory_space=pltpu.VM...  27.5 us
    pallas_call x1, Pallas kernels, inverse_gains(): pl.pallas_call(gains_kernel, in_specs=[hbm, hbm, hbm], out_specs=[vmem, v...  19.9 us
    pallas_call x1, Pallas kernels, calibrated_sums(): pl.pallas_call(sums_kernel, in_specs=[hbm, hbm, vmem, vmem, vmem], out_sp...  5.31 us

profile of v6, /device:TPU:1, one launch (start us, length us, event | category | flops | bytes accessed | tf_op | source)
XLA Modules:
  0.0 53.4 jit_solution(6670717018552998763)
XLA Ops:
  0.0 19.9 %gains.1 = (f32[2,8,512]{2,1,0:T(8,128)S(1)}, bf16[8,2,512,512]{3,2,1,0:T(8,128)(2,1)S(1)}, f32[4,2,512,512]{3,2,1,0:T(8,128)S(1)}) custom-call(s32[2]{0:T(128)} %width_hbm.1, bf16[8,2,512,512]{3,2,1,0:T(8,128)(2,1)} %bitcast.3, bf16[8,2,512,512]{3,2,1,0:T(8,128)(2,1)} %bitcast.4), custom_call_target="tpu_custom_call" | custom-call | tf_op jit(solution)/shard_map/gains/pallas_call | solution.py:228
  19.9 0.0 copy-start
  19.9 0.0 copy-start.1
  19.9 5.3 %sums.1.sums_ref = f32[64,128,256]{2,1,0:T(8,128)S(1)} custom-call(s32[2,16]{1,0:T(2,128)} %weight_hbm.1, s32[8,16]{1,0:T(8,128)} %bitcast.5, f32[2,8,512]{2,1,0:T(8,128)S(1)} %get-tuple-element.8.inv_ref, bf16[8,2,512,512]{3,2,1,0:T(8,128)(2,1)S(1)} %get-tuple-element.9.vis_ref, f32[4,2,512,512]{3,2,1,0:T(8,128)S(1)} %get-tuple-element.10.wide_ref), custom_call_target="tpu_custom_call" | custom-call | tf_op jit(solution)/shard_map/sums/pallas_call | solution.py:334
  25.2 0.0 copy-done
  25.2 0.0 copy-done.1
  25.2 27.5 %beams.1 = f32[128,256]{1,0:T(8,128)S(1)} custom-call(bf16[8,256,128]{2,1,0:T(8,128)(2,1)S(1)} %copy-done, bf16[8,256,128]{2,1,0:T(8,128)(2,1)S(1)} %copy-done.1, f32[64,128,256]{2,1,0:T(8,128)S(1)} %sums.1.sums_ref), custom_call_target="tpu_custom_call" | custom-call | tf_op jit(solution)/shard_map/beams/pallas_call | solution.py:617
  52.7 0.7 %copy.9 = f32[128,256]{1,0:T(8,128)} copy(f32[128,256]{1,0:T(8,128)S(1)} %beams.1) | data formatting | bytes 262144
Async XLA Ops:
  19.9 5.3 %copy-start = (bf16[8,256,128]{2,1,0:T(8,128)(2,1)S(1)}, bf16[8,256,128]{2,1,0:T(8,128)(2,1)}, u32[]{:S(2)}) copy-start(bf16[8,256,128]{2,1,0:T(8,128)(2,1)} %left_ref.1) | copy-start | bytes 1572868
  19.9 5.3 %copy-start.1 = (bf16[8,256,128]{2,1,0:T(8,128)(2,1)S(1)}, bf16[8,256,128]{2,1,0:T(8,128)(2,1)}, u32[]{:S(2)}) copy-start(bf16[8,256,128]{2,1,0:T(8,128)(2,1)} %right_ref.1) | copy-start | bytes 1572868
